TPU v7x, 32 devices: a whole 2x2x4 slice. The times are simulated.
32 devices in a mesh: grp: 2 (over y), sec: 16 (over z, x, core).
Axes of the slice: x: 2, y: 2, z: 4, core: 2. Of those that a mesh axis runs over, the one named last changes fastest.
Arguments:
- vectors: bfloat16 [3, 64, 64, 1024], P(None, ('grp', 'sec')), parts along dimension 1, may hold values from -6 to 6
- left_env: bfloat16 [64, 64, 128], P(('grp', 'sec')), parts along dimension 0, may hold values from -0.75 to 0.75
- right_env: bfloat16 [64, 64, 128], P(('grp', 'sec')), parts along dimension 0, may hold values from -0.5 to 0.5
- target_device: int32 [64, 16, 1], P(('grp', 'sec')), parts along dimension 0, may hold values from 0 to 15; in each aligned block of 32 rows (0 to 31, 32 to 63, ..., all dimensions but the last counted through in order) at most 4 rows name the same one
- target_slot: int32 [64, 16], P(('grp', 'sec')), parts along dimension 0, may hold values from 0 to 1
Outputs:
- products: bfloat16 [3, 64, 64, 1024], P(None, ('grp', 'sec')), parts along dimension 1
There are 2 independent parts, one for each index of `grp`. A program takes and returns all parts, laid end to end along the dimension named above; each array names one. Nothing has to cross between parts.
Inputs may be any that keep to these rules, and one draw needn't show every extreme that they name: `target_device`: among the blocks of one device no device is named more than 4 times, and in some device's blocks one device is named exactly 4 times.
All inputs are finite; a program needn't handle non-finite values.
Results may differ from a plain program's by a relative error of at most 0.0049.
Values may be sent and summed in bfloat16 or wider, within the bound.
No kernel may reach another device: no remote copies, remote signals or barrier semaphores. Data moves between devices by JAX's collectives and lax.ppermute only.
A program may use at most 128 MiB of HBM per device.

v0:
```python
import jax
import jax.numpy as jnp
from jax import lax
from jax.sharding import PartitionSpec as P


def body(vectors, left_env, right_env, target_device, target_slot):
    peers = lax.axis_size("sec")
    vecs, secs, width, wide = vectors.shape
    pairs = wide // width
    terms = left_env.shape[2] // width
    rows = secs * pairs
    capacity = max(2, 2 * rows // peers)
    dest = target_device.reshape(rows)
    slot_ids = target_slot.reshape(rows)
    onehot = (dest[:, None] == jnp.arange(peers, dtype=jnp.int32)[None, :]).astype(jnp.int32)
    before = jnp.cumsum(onehot, axis=0) - onehot
    rank = jnp.sum(before * onehot, axis=1)
    places = dest * capacity + rank
    row_of = (
        jnp.full((peers * capacity,), -1, jnp.int32)
        .at[places]
        .set(jnp.arange(rows, dtype=jnp.int32))
    )
    filled = row_of >= 0
    safe_row = jnp.maximum(row_of, 0)
    lefts = left_env.reshape(secs, width, terms, width)
    pieces = vectors.reshape(vecs, secs, width, pairs, width)
    mixed = jnp.einsum("amwi,vampj->apviwj", lefts, pieces, preferred_element_type=jnp.float32)
    mixed = mixed.astype(jnp.bfloat16).reshape(rows, vecs, width, terms * width)
    wanted = jnp.where(filled, jnp.take(slot_ids, safe_row), -1).reshape(peers, capacity)
    outgoing = jnp.take(mixed, safe_row, axis=0)
    outgoing = jnp.where(filled[:, None, None, None], outgoing, jnp.zeros_like(outgoing))
    outgoing = outgoing.reshape(peers, capacity, vecs, width, terms * width)
    blocks = lax.all_to_all(outgoing, "sec", split_axis=0, concat_axis=0, tiled=True)
    needed = lax.all_to_all(wanted, "sec", split_axis=0, concat_axis=0, tiled=True)
    chosen = jnp.take(right_env, jnp.maximum(needed, 0), axis=0)
    result = jnp.einsum("ncviq,nckq->ncvik", blocks, chosen, preferred_element_type=jnp.float32)
    back = lax.all_to_all(
        result.astype(jnp.bfloat16), "sec", split_axis=0, concat_axis=0, tiled=True
    )
    back = back.reshape(peers * capacity, vecs, width, width)
    finished = jnp.take(back, places, axis=0)
    finished = finished.reshape(secs, pairs, vecs, width, width)
    finished = jnp.transpose(finished, (2, 0, 3, 1, 4))
    return finished.reshape(vecs, secs, width, pairs * width)


def solution(mesh):
    return jax.shard_map(
        body,
        mesh=mesh,
        in_specs=(
            P(None, ("grp", "sec"), None, None),
            P(("grp", "sec"), None, None),
            P(("grp", "sec"), None, None),
            P(("grp", "sec"), None, None),
            P(("grp", "sec"), None),
        ),
        out_specs=P(None, ("grp", "sec"), None, None),
        check_vma=False,
    )
```

profile of v0, /device:TPU:15, one launch (start us, length us, event | category | flops | bytes accessed | tf_op | source)
XLA Modules:
  0.0 171.2 jit_solution(9700791833936639812)
XLA Ops:
  0.0 0.0 copy-start
  0.0 0.5 broadcast.115
  0.5 1.3 fusion.12
  1.9 0.1 reshape.102
  1.9 0.1 fusion.6
  2.0 0.1 reduce_window_sum.11
  2.1 0.2 select_reduce_fusion
  2.3 0.1 mul.29
  2.3 0.7 scatter_custom_fusion
  3.1 0.8 reshape.106
  3.8 0.8 gather_fusion.1
  4.6 0.7 all_to_all.13
  5.3 6.6 %all-to-all-start.1 = ((s32[16,1,4]{2,1,0:T(1,128)}), s32[16,1,4]{2,1,0:T(1,128)S(1)}, u32[]{:S(2)}, u32[]{:S(2)}) async-start(s32[16,1,4]{2,1,0:T(1,128)} %bitcast.9), calls=%async_computation.1 | async-start | bytes 16384 | tf_op jit(solution)/shard_map/all_to_all | solution.py:36
  11.9 2.5 %copy.27 = bf16[3,2,64,1024]{2,3,0,1:T(8,128)(2,1)} copy(bf16[3,2,64,1024]{3,2,1,0:T(8,128)(2,1)} %param.5) | data formatting | bytes 1572864 | tf_op jit(solution)/shard_map/reshape | solution.py:28
  14.3 0.8 reshape.104
  15.2 2.4 %convert_bitcast_fusion = bf16[2,16,3,64,2,64]{3,5,4,1,2,0:T(8,128)(2,1)S(1)} fusion(bf16[3,2,64,16,64,1]{2,4,5,3,0,1:T(8,128)(2,1)} %bitcast.35, bf16[2,64,2,64,1,1]{3,2,1,0,5,4:T(2,128)(2,1)S(1)} %bitcast.38), kind=kOutput, calls=%fused_computation.6 | convolution fusion | flops 101449728 | bytes 2392064 | tf_op jit(solution)/shard_map/amwi,vampj->apviwj/dot_general | solution.py:29
  17.6 5.5 %copy.19 = bf16[2,16,3,64,2,64]{5,4,3,2,1,0:T(2,128)(2,1)} copy(bf16[2,16,3,64,2,64]{3,5,4,1,2,0:T(8,128)(2,1)S(1)} %convert_bitcast_fusion) | data formatting | bytes 3145728 | tf_op jit(solution)/shard_map/convert_element_type | solution.py:30
  23.1 5.3 %reshape.105 = bf16[32,3,64,128]{3,2,1,0:T(8,128)(2,1)S(1)} reshape(bf16[2,16,3,64,2,64]{5,4,3,2,1,0:T(2,128)(2,1)} %copy.19) | data formatting | bytes 3145728 | tf_op jit(solution)/shard_map/reshape | solution.py:30
  28.5 2.7 %gather_fusion = bf16[64,3,64,128]{3,2,1,0:T(8,128)(2,1)} fusion(bf16[32,3,64,128]{3,2,1,0:T(8,128)(2,1)S(1)} %reshape.105, s32[1024]{0:T(1024)S(1)} %pad_clamp_fusion.2), kind=kCustom, calls=%fused_computation | custom fusion | bytes 6291712 | tf_op jit(solution)/shard_map/jit(_take)/gather | solution.py:32
  31.1 0.1 broadcast_in_dim.63
  31.2 0.1 broadcast_in_dim.65
  31.3 4.0 %select_select_fusion = bf16[16,4,3,64,128]{4,3,2,1,0:T(8,128)(2,1)} fusion(bf16[16,4,3,64,128]{4,3,2,1,0:T(8,128)(2,1)} %bitcast.33, pred[16,4]{1,0:T(8,128)(4,1)S(1)} %broadcast_in_dim.65, pred[16,4]{1,0:T(8,128)(4,1)S(1)} %broadcast_in_dim.63), kind=kLoop, calls=%fused_computation.5 | loop fusion | flops 3145728 | bytes 6291584 | tf_op jit(solution)/shard_map/jit(_where)/select_n | solution.py:33
  35.3 0.0 all-to-all-done.1
  35.3 6.0 %all-to-all-start = ((bf16[16,4,3,64,128]{4,3,2,1,0:T(8,128)(2,1)}), bf16[16,4,3,64,128]{4,3,2,1,0:T(8,128)(2,1)S(1)}, u32[]{:S(2)}, u32[]{:S(2)}) async-start(bf16[16,4,3,64,128]{4,3,2,1,0:T(8,128)(2,1)} %select_select_fusion), calls=%async_computation | async-start | bytes 6291456 | tf_op jit(solution)/shard_map/all_to_all | solution.py:35
  41.4 0.1 reshape.127
  41.5 0.1 copy.21
  41.6 0.1 copy.22
  41.7 0.0 copy-done
  41.7 1.7 gather_fusion.2
  43.4 67.9 %all-to-all-done = bf16[16,4,3,64,128]{4,3,2,1,0:T(8,128)(2,1)S(1)} async-done(((bf16[16,4,3,64,128]{4,3,2,1,0:T(8,128)(2,1)}), bf16[16,4,3,64,128]{4,3,2,1,0:T(8,128)(2,1)S(1)}, u32[]{:S(2)}, u32[]{:S(2)}) %all-to-all-start) | async-done | bytes 3145760 | tf_op jit(solution)/shard_map/all_to_all | solution.py:35
  111.2 3.9 %convolution_convert_fusion = bf16[16,4,3,64,64]{4,3,2,1,0:T(8,128)(2,1)} fusion(bf16[16,4,3,64,128]{4,3,2,1,0:T(8,128)(2,1)S(1)} %all-to-all-done, bf16[16,4,64,128]{3,2,1,0:T(8,128)(2,1)} %bitcast.37, pred[16,4]{1,0:T(8,128)(4,1)S(1)} %copy.22), kind=kOutput, calls=%fused_computation.7 | convolution fusion | flops 202637312 | bytes 5767232 | tf_op jit(solution)/shard_map/ncviq,nckq->ncvik/dot_general | solution.py:38
  115.2 4.9 %reshape.177 = bf16[16,2,24576]{2,1,0:T(2,128)(2,1)} reshape(bf16[16,4,3,64,64]{4,3,2,1,0:T(8,128)(2,1)} %convolution_convert_fusion) | data formatting | bytes 3145728
  120.1 4.9 %all-to-all-start.2 = ((bf16[16,2,24576]{2,1,0:T(2,128)(2,1)}), bf16[16,2,24576]{2,1,0:T(2,128)(2,1)}, u32[]{:S(2)}, u32[]{:S(2)}) async-start(bf16[16,2,24576]{2,1,0:T(2,128)(2,1)} %reshape.177), calls=%async_computation.2 | async-start | bytes 3145728 | tf_op jit(solution)/shard_map/all_to_all | solution.py:39
  125.0 0.1 reduce_sum.14
  125.1 36.2 %all-to-all-done.2 = bf16[16,2,24576]{2,1,0:T(2,128)(2,1)} async-done(((bf16[16,2,24576]{2,1,0:T(2,128)(2,1)}), bf16[16,2,24576]{2,1,0:T(2,128)(2,1)}, u32[]{:S(2)}, u32[]{:S(2)}) %all-to-all-start.2) | async-done | bytes 1572896 | tf_op jit(solution)/shard_map/all_to_all | solution.py:39
  161.3 3.8 %reshape.178 = bf16[16,4,3,64,64]{4,3,2,1,0:T(8,128)(2,1)S(1)} reshape(bf16[16,2,24576]{2,1,0:T(2,128)(2,1)} %all-to-all-done.2) | data formatting | bytes 3145728
  165.1 1.9 %gather_fusion.3 = bf16[32,3,64,64]{3,2,1,0:T(8,128)(2,1)} fusion(bf16[64,3,64,64]{3,2,1,0:T(8,128)(2,1)S(1)} %bitcast.34, s32[1024]{0:T(1024)S(1)} %pad_clamp_fusion), kind=kCustom, calls=%fused_computation.3 | custom fusion | bytes 1572992 | tf_op jit(solution)/shard_map/jit(_take)/gather | solution.py:43
  167.0 2.4 %fusion = bf16[3,2,64,16,64]{4,3,2,1,0:T(8,128)(2,1)S(1)} fusion(bf16[2,16,3,64,64]{4,3,2,1,0:T(8,128)(2,1)} %bitcast.36, pred[2,16]{1,0:T(4,128)(4,1)S(1)} %compare_and_fusion), kind=kLoop, calls=%fused_computation.9 | loop fusion | flops 393216 | bytes 1572896 | tf_op jit(solution)/shard_map/transpose | solution.py:45
  169.4 1.9 %reshape.108 = bf16[3,2,64,1024]{3,2,1,0:T(8,128)(2,1)} reshape(bf16[3,2,64,16,64]{4,3,2,1,0:T(8,128)(2,1)S(1)} %fusion) | data formatting | bytes 1572864 | tf_op jit(solution)/shard_map/reshape | solution.py:46
  (11 shorter events, 0.1 us)
Async XLA Ops:
  0.0 41.7 %copy-start = (bf16[2,64,128]{2,1,0:T(8,128)(2,1)S(1)}, bf16[2,64,128]{2,1,0:T(8,128)(2,1)}, u32[]{:S(2)}) copy-start(bf16[2,64,128]{2,1,0:T(8,128)(2,1)} %param.7) | copy-start | bytes 98308
  5.3 30.0 %all-to-all-start.1 = ((s32[16,1,4]{2,1,0:T(1,128)}), s32[16,1,4]{2,1,0:T(1,128)S(1)}, u32[]{:S(2)}, u32[]{:S(2)}) async-start(s32[16,1,4]{2,1,0:T(1,128)} %bitcast.9), calls=%async_computation.1 | async-start | bytes 16384 | tf_op jit(solution)/shard_map/all_to_all | solution.py:36
  35.3 75.9 %all-to-all-start = ((bf16[16,4,3,64,128]{4,3,2,1,0:T(8,128)(2,1)}), bf16[16,4,3,64,128]{4,3,2,1,0:T(8,128)(2,1)S(1)}, u32[]{:S(2)}, u32[]{:S(2)}) async-start(bf16[16,4,3,64,128]{4,3,2,1,0:T(8,128)(2,1)} %select_select_fusion), calls=%async_computation | async-start | bytes 6291456 | tf_op jit(solution)/shard_map/all_to_all | solution.py:35
  120.1 41.2 %all-to-all-start.2 = ((bf16[16,2,24576]{2,1,0:T(2,128)(2,1)}), bf16[16,2,24576]{2,1,0:T(2,128)(2,1)}, u32[]{:S(2)}, u32[]{:S(2)}) async-start(bf16[16,2,24576]{2,1,0:T(2,128)(2,1)} %reshape.177), calls=%async_computation.2 | async-start | bytes 3145728 | tf_op jit(solution)/shard_map/all_to_all | solution.py:39
where the time goes:
time: 172 us; the launch traced here: 171 us
  waiting for transfers between devices  104 us (60%)
  local copies, waits for them, and re-layouts  35.1 us (20%)
  starting transfers between devices  17.5 us (10%)
  other arithmetic  8.14 us (5%)
  matrix products  6.3 us (4%)
    all_to_all x1, waiting for transfers between devices, body(): lax.all_to_all(outgoing, 'sec', split_axis=0, concat_axis=0, tiled=True)  67.9 us
    all_to_all x1, waiting for transfers between devices, body(): lax.all_to_all(result.astype(jnp.bfloat16), 'sec', split_axis=0, concat_a...  36.2 us
    unnamed x5, local copies, waits for them, and re-layouts  9.22 us
    all_to_all x1, starting transfers between devices, body(): lax.all_to_all(wanted, 'sec', split_axis=0, concat_axis=0, tiled=True)  6.55 us
    all_to_all x1, starting transfers between devices, body(): lax.all_to_all(outgoing, 'sec', split_axis=0, concat_axis=0, tiled=True)  6.02 us
    convert_element_type x1, local copies, waits for them, and re-layouts, body(): mixed = mixed.astype(jnp.bfloat16).reshape(rows, vecs, width, terms * width)  5.55 us
    reshape x1, local copies, waits for them, and re-layouts, body(): mixed = mixed.astype(jnp.bfloat16).reshape(rows, vecs, width, terms * width)  5.34 us
    all_to_all x1, starting transfers between devices, body(): lax.all_to_all(result.astype(jnp.bfloat16), 'sec', split_axis=0, concat_a...  4.9 us
  transfers between devices with their start and end apart: 3, of which 2 were waited for; matrix products, arithmetic and copies ran while one was open for 15% of the time, Pallas kernels for 0%

commit v1 on v0

v1 whole, which is shorter than its diff:
```python
import functools

import jax
import jax.numpy as jnp
from jax import lax
from jax.experimental import pallas as pl
from jax.experimental.pallas import tpu as pltpu
from jax.sharding import PartitionSpec as P


def phases_of(peers):
    bits = []
    bit = peers // 2
    while bit > 1:
        bits.append(bit)
        bit //= 2
    groups = [bits[:1]] if bits else []
    rest = bits[1:]
    while rest:
        groups.append(rest[:2])
        rest = rest[2:]
    if peers > 1:
        groups.append([1])
    return groups


def combos(group):
    sums = [0]
    for bit in group:
        sums = sums + [s ^ bit for s in sums]
    return sums[1:]


def place_of(apart, peers):
    place = jnp.zeros_like(apart)
    at = 0
    for group in phases_of(peers):
        for bit in group:
            place = place + (((apart // bit) % 2) << at)
            at += 1
    return place


def hop(x, apart, peers):
    return lax.ppermute(x, "sec", [(i, i ^ apart) for i in range(peers)])


def mix_kernel(left_ref, vec_ref, mixed_ref):
    vecs, secs, width, _ = vec_ref.shape
    terms = left_ref.shape[2] // width
    for a in range(secs):
        turned = left_ref[a].T
        for v in range(vecs):
            both = jnp.dot(turned, vec_ref[v, a], preferred_element_type=jnp.float32).astype(jnp.bfloat16)
            for w in range(terms):
                mixed_ref[a, w, v * width : (v + 1) * width, :] = both[w * width : (w + 1) * width]


def close_kernel(at_ref, mixed_ref, env_ref, out_ref, done_ref, sems):
    secs, terms, tall, wide = mixed_ref.shape
    width = env_ref.shape[1]
    pairs = wide // width
    vecs = tall // width
    lane = lax.broadcasted_iota(jnp.int32, (width, 2 * width), 1)
    low = lane < width
    copies = []
    for a in range(secs):
        for p in range(0, pairs, 2):
            first = env_ref[at_ref[a, p]]
            second = env_ref[at_ref[a, p + 1]]
            zero = jnp.zeros_like(first)
            top = [jnp.where(low, first, zero), jnp.where(low, pltpu.roll(first, width, 1), zero)]
            bottom = [jnp.where(low, zero, pltpu.roll(second, width, 1)), jnp.where(low, zero, second)]
            weights = jnp.concatenate([jnp.concatenate(top, 1), jnp.concatenate(bottom, 1)], 0)
            cols = slice(p * width, (p + 2) * width)
            rows = jnp.concatenate([mixed_ref[a, w, :, cols] for w in range(terms)], 1)
            block = lax.dot_general(
                rows, weights, (((1,), (1,)), ((), ())), preferred_element_type=jnp.float32
            ).astype(jnp.bfloat16)
            for v in range(vecs):
                done_ref[v, a, :, cols] = block[v * width : (v + 1) * width]
        copy = pltpu.make_async_copy(done_ref.at[:, a], out_ref.at[:, a], sems.at[a])
        copy.start()
        copies.append(copy)
    for copy in copies:
        copy.wait()


def body(vectors, left_env, right_env, target_device, target_slot):
    peers = lax.axis_size("sec")
    vecs, secs, width, wide = vectors.shape
    pairs = wide // width
    terms = left_env.shape[2] // width
    me = lax.axis_index("sec")
    dest = target_device.reshape(secs, pairs)
    at = place_of(dest ^ me, peers) * secs + target_slot
    mixed = pl.pallas_call(
        mix_kernel,
        out_shape=jax.ShapeDtypeStruct((secs, terms, vecs * width, wide), jnp.bfloat16),
        cost_estimate=pl.CostEstimate(
            flops=2 * vecs * secs * terms * width * width * wide,
            bytes_accessed=6 * vecs * secs * width * wide,
            transcendentals=0,
        ),
    )(left_env, vectors)
    env = right_env
    for group in phases_of(peers):
        env = jnp.concatenate([env] + [hop(env, s, peers) for s in combos(group)], 0)
    return pl.pallas_call(
        close_kernel,
        out_shape=jax.ShapeDtypeStruct(vectors.shape, jnp.bfloat16),
        in_specs=[
            pl.BlockSpec(memory_space=pltpu.SMEM),
            pl.BlockSpec(memory_space=pltpu.VMEM),
            pl.BlockSpec(memory_space=pltpu.VMEM),
        ],
        out_specs=pl.BlockSpec(memory_space=pl.ANY),
        scratch_shapes=[pltpu.VMEM(vectors.shape, jnp.bfloat16), pltpu.SemaphoreType.DMA((secs,))],
        cost_estimate=pl.CostEstimate(
            flops=2 * vecs * secs * terms * width * width * wide,
            bytes_accessed=6 * vecs * secs * width * wide,
            transcendentals=0,
        ),
    )(at, mixed, env)


def solution(mesh):
    return jax.shard_map(
        body,
        mesh=mesh,
        in_specs=(
            P(None, ("grp", "sec"), None, None),
            P(("grp", "sec"), None, None),
            P(("grp", "sec"), None, None),
            P(("grp", "sec"), None, None),
            P(("grp", "sec"), None),
        ),
        out_specs=P(None, ("grp", "sec"), None, None),
        check_vma=False,
    )
```

time: 172 us -> 22.4 us (0.13)
  the two profiles are of different devices: /device:TPU:15 before, /device:TPU:0 now
where the time goes in v1:
time: 22.4 us; the launch traced here: 22.1 us
  starting transfers between devices  7.66 us (34%)
  Pallas kernels  5.84 us (26%)
  waiting for transfers between devices  5.55 us (25%)
  local copies, waits for them, and re-layouts  1.74 us (8%)
  other arithmetic  1.28 us (6%)
    ppermute x5, starting transfers between devices, hop(): return lax.ppermute(x, 'sec', [(i, i ^ apart) for i in range(peers)])  7.66 us
    ppermute x5, waiting for transfers between devices, hop(): return lax.ppermute(x, 'sec', [(i, i ^ apart) for i in range(peers)])  5.55 us
    pallas_call x1, Pallas kernels, body(): pl.pallas_call(close_kernel, out_shape=jax.ShapeDtypeStruct(vectors.shape...  2.95 us
    pallas_call x1, Pallas kernels, body(): pl.pallas_call(mix_kernel, out_shape=jax.ShapeDtypeStruct((secs, terms, v...  2.9 us
    unnamed x8, local copies, waits for them, and re-layouts  1.68 us
    xor x1, other arithmetic, body(): at = place_of(dest ^ me, peers) * secs + target_slot  0.68 us
    add x1, other arithmetic, body(): at = place_of(dest ^ me, peers) * secs + target_slot  0.6 us
  transfers between devices with their start and end apart: 5, of which 3 were waited for; matrix products, arithmetic and copies ran while one was open for 10% of the time, Pallas kernels for 13%

profile of v1, /device:TPU:0, one launch (start us, length us, event | category | flops | bytes accessed | tf_op | source)
XLA Modules:
  0.0 22.1 jit_solution(12869891314771071459)
XLA Ops:
  0.0 4.0 %collective-permute-start = (bf16[2,64,128]{2,1,0:T(8,128)(2,1)}, bf16[2,64,128]{2,1,0:T(8,128)(2,1)S(1)}, u32[]{:S(2)}, u32[]{:S(2)}) collective-permute-start(bf16[2,64,128]{2,1,0:T(8,128)(2,1)} %param.7), channel_id=1, source_target_pairs={{0,8},{1,9},{2,10},{3,11},{4,12},{5,13},{6,14},{7,15},{8,0},{9,1},... | collective-permute-start | bytes 98312 | tf_op jit(solution)/shard_map/ppermute | solution.py:45
  4.0 0.8 %constant_dynamic-update-slice_fusion.6 = (bf16[16,64,128]{2,1,0:T(8,128)(2,1)S(1)}, bf16[4,64,128]{2,1,0:T(8,128)(2,1)S(1)}, bf16[32,64,128]{2,1,0:T(8,128)(2,1)S(1)}) fusion(bf16[2,64,128]{2,1,0:T(8,128)(2,1)} %param.7), kind=kLoop, calls=%fused_computation.6 | loop fusion | bytes 131072
  4.8 0.0 copy-start.1
  4.9 1.6 %collective-permute-done = bf16[2,64,128]{2,1,0:T(8,128)(2,1)S(1)} collective-permute-done((bf16[2,64,128]{2,1,0:T(8,128)(2,1)}, bf16[2,64,128]{2,1,0:T(8,128)(2,1)S(1)}, u32[]{:S(2)}, u32[]{:S(2)}) %collective-permute-start) | collective-permute-done | bytes 32800 | tf_op jit(solution)/shard_map/ppermute | solution.py:45
  6.5 1.6 %collective-permute-start.1 = (bf16[4,64,128]{2,1,0:T(8,128)(2,1)S(1)}, bf16[4,64,128]{2,1,0:T(8,128)(2,1)S(1)}, u32[]{:S(2)}, u32[]{:S(2)}) collective-permute-start(bf16[4,64,128]{2,1,0:T(8,128)(2,1)S(1)} %get-tuple-element.13), channel_id=1, source_target_pairs={{0,4},{1,5},{2,6},{3,7},{4,0},{5,1},{6,2},{7,3},{8,12},{9,13},{10,... | collective-permute-start | bytes 196616 | tf_op jit(solution)/shard_map/ppermute | solution.py:45
  8.1 1.6 %collective-permute-start.3 = (bf16[4,64,128]{2,1,0:T(8,128)(2,1)S(1)}, bf16[4,64,128]{2,1,0:T(8,128)(2,1)S(1)}, u32[]{:S(2)}, u32[]{:S(2)}) collective-permute-start(bf16[4,64,128]{2,1,0:T(8,128)(2,1)S(1)} %get-tuple-element.13), channel_id=1, source_target_pairs={{0,6},{1,7},{2,4},{3,5},{4,2},{5,3},{6,0},{7,1},{8,14},{9,15},{10,... | collective-permute-start | bytes 196616 | tf_op jit(solution)/shard_map/ppermute | solution.py:45
  9.7 0.3 %collective-permute-start.2 = (bf16[4,64,128]{2,1,0:T(8,128)(2,1)S(1)}, bf16[4,64,128]{2,1,0:T(8,128)(2,1)S(1)}, u32[]{:S(2)}, u32[]{:S(2)}) collective-permute-start(bf16[4,64,128]{2,1,0:T(8,128)(2,1)S(1)} %get-tuple-element.13), channel_id=1, source_target_pairs={{0,2},{1,3},{2,0},{3,1},{4,6},{5,7},{6,4},{7,5},{8,10},{9,11},{10,... | collective-permute-start | bytes 196616 | tf_op jit(solution)/shard_map/ppermute | solution.py:45
  10.1 1.4 %collective-permute-done.1 = bf16[4,64,128]{2,1,0:T(8,128)(2,1)S(1)} collective-permute-done((bf16[4,64,128]{2,1,0:T(8,128)(2,1)S(1)}, bf16[4,64,128]{2,1,0:T(8,128)(2,1)S(1)}, u32[]{:S(2)}, u32[]{:S(2)}) %collective-permute-start.1) | collective-permute-done | bytes 65568 | tf_op jit(solution)/shard_map/ppermute | solution.py:45
  11.5 2.5 %collective-permute-done.2 = bf16[4,64,128]{2,1,0:T(8,128)(2,1)S(1)} collective-permute-done((bf16[4,64,128]{2,1,0:T(8,128)(2,1)S(1)}, bf16[4,64,128]{2,1,0:T(8,128)(2,1)S(1)}, u32[]{:S(2)}, u32[]{:S(2)}) %collective-permute-start.2) | collective-permute-done | bytes 65568 | tf_op jit(solution)/shard_map/ppermute | solution.py:45
  14.0 0.0 collective-permute-done.3
  14.1 0.1 collective-permute-start.4
  14.2 0.7 %broadcast_xor_fusion = s32[2,16,1]{1,2,0:T(1,128)S(1)} fusion(s32[2,16,1]{1,2,0:T(1,128)} %param.8, s32[]{:T(128)S(6)} %axis_index.12), kind=kLoop, calls=%fused_computation.44 | loop fusion | flops 32 | bytes 260 | tf_op jit(solution)/shard_map/xor | solution.py:96
  14.9 2.9 %shard_map.55.mixed_ref = bf16[2,2,192,1024]{3,2,1,0:T(8,128)(2,1)} custom-call(bf16[2,64,128]{2,1,0:T(8,128)(2,1)} %left_ref.1, bf16[3,2,64,1024]{3,2,1,0:T(8,128)(2,1)} %vec_ref.1), custom_call_target="tpu_custom_call" | custom-call | flops 100663296 | bytes 2359296 | tf_op jit(solution)/shard_map/pallas_call | solution.py:97
  17.8 0.0 copy-done.1
  17.8 0.6 %multiply_add_fusion.at_ref = s32[2,16]{1,0:T(2,128)} fusion(s32[2,16]{1,0:T(2,128)S(1)} %copy-done.1, s32[2,16]{1,0:T(2,128)S(1)} %bitcast.1), kind=kLoop, calls=%fused_computation.43 | loop fusion | flops 2592 | bytes 384 | tf_op jit(solution)/shard_map/add | solution.py:96
  18.4 0.0 collective-permute-done.4
  18.4 0.0 copy-start
  18.4 0.8 %copy-done = bf16[32,64,128]{2,1,0:T(8,128)(2,1)} copy-done((bf16[32,64,128]{2,1,0:T(8,128)(2,1)}, bf16[32,64,128]{2,1,0:T(8,128)(2,1)S(1)}, u32[]{:S(2)}) %copy-start) | copy-done | bytes 524312
  19.2 2.9 %shard_map.56 = bf16[3,2,64,1024]{3,2,1,0:T(8,128)(2,1)} custom-call(s32[2,16]{1,0:T(2,128)} %multiply_add_fusion.at_ref, bf16[2,2,192,1024]{3,2,1,0:T(8,128)(2,1)} %shard_map.55.mixed_ref, bf16[32,64,128]{2,1,0:T(8,128)(2,1)} %copy-done), custom_call_target="tpu_custom_call" | custom-call | flops 100663296 | bytes 2359296 | tf_op jit(solution)/shard_map/pallas_call | solution.py:109
  (5 shorter events, 0.1 us)
Async XLA Ops:
  0.0 6.5 %collective-permute-start = (bf16[2,64,128]{2,1,0:T(8,128)(2,1)}, bf16[2,64,128]{2,1,0:T(8,128)(2,1)S(1)}, u32[]{:S(2)}, u32[]{:S(2)}) collective-permute-start(bf16[2,64,128]{2,1,0:T(8,128)(2,1)} %param.7), channel_id=1, source_target_pairs={{0,8},{1,9},{2,10},{3,11},{4,12},{5,13},{6,14},{7,15},{8,0},{9,1},... | collective-permute-start | bytes 98312 | tf_op jit(solution)/shard_map/ppermute | solution.py:45
  4.8 12.9 %copy-start.1 = (s32[2,16]{1,0:T(2,128)S(1)}, s32[2,16]{1,0:T(2,128)}, u32[]{:S(2)}) copy-start(s32[2,16]{1,0:T(2,128)} %param.9) | copy-start | bytes 388
  6.5 5.0 %collective-permute-start.1 = (bf16[4,64,128]{2,1,0:T(8,128)(2,1)S(1)}, bf16[4,64,128]{2,1,0:T(8,128)(2,1)S(1)}, u32[]{:S(2)}, u32[]{:S(2)}) collective-permute-start(bf16[4,64,128]{2,1,0:T(8,128)(2,1)S(1)} %get-tuple-element.13), channel_id=1, source_target_pairs={{0,4},{1,5},{2,6},{3,7},{4,0},{5,1},{6,2},{7,3},{8,12},{9,13},{10,... | collective-permute-start | bytes 196616 | tf_op jit(solution)/shard_map/ppermute | solution.py:45
  8.1 5.9 %collective-permute-start.3 = (bf16[4,64,128]{2,1,0:T(8,128)(2,1)S(1)}, bf16[4,64,128]{2,1,0:T(8,128)(2,1)S(1)}, u32[]{:S(2)}, u32[]{:S(2)}) collective-permute-start(bf16[4,64,128]{2,1,0:T(8,128)(2,1)S(1)} %get-tuple-element.13), channel_id=1, source_target_pairs={{0,6},{1,7},{2,4},{3,5},{4,2},{5,3},{6,0},{7,1},{8,14},{9,15},{10,... | collective-permute-start | bytes 196616 | tf_op jit(solution)/shard_map/ppermute | solution.py:45
  9.7 4.3 %collective-permute-start.2 = (bf16[4,64,128]{2,1,0:T(8,128)(2,1)S(1)}, bf16[4,64,128]{2,1,0:T(8,128)(2,1)S(1)}, u32[]{:S(2)}, u32[]{:S(2)}) collective-permute-start(bf16[4,64,128]{2,1,0:T(8,128)(2,1)S(1)} %get-tuple-element.13), channel_id=1, source_target_pairs={{0,2},{1,3},{2,0},{3,1},{4,6},{5,7},{6,4},{7,5},{8,10},{9,11},{10,... | collective-permute-start | bytes 196616 | tf_op jit(solution)/shard_map/ppermute | solution.py:45
  14.1 4.3 %collective-permute-start.4 = (bf16[16,64,128]{2,1,0:T(8,128)(2,1)S(1)}, bf16[16,64,128]{2,1,0:T(8,128)(2,1)S(1)}, u32[]{:S(2)}, u32[]{:S(2)}) collective-permute-start(bf16[16,64,128]{2,1,0:T(8,128)(2,1)S(1)} %get-tuple-element.5), channel_id=1, source_target_pairs={{0,1},{1,0},{2,3},{3,2},{4,5},{5,4},{6,7},{7,6},{8,9},{9,8},{10,11... | collective-permute-start | bytes 786440 | tf_op jit(solution)/shard_map/ppermute | solution.py:45
  18.4 0.8 %copy-start = (bf16[32,64,128]{2,1,0:T(8,128)(2,1)}, bf16[32,64,128]{2,1,0:T(8,128)(2,1)S(1)}, u32[]{:S(2)}) copy-start(bf16[32,64,128]{2,1,0:T(8,128)(2,1)S(1)} %constant_dynamic-update-slice_fusion.7.env_ref) | copy-start | bytes 1572868

commit v2 on v1

--- a/solution.py
+++ b/solution.py
@@ -32,11 +32,11 @@
 
 
 def place_of(apart, peers):
-    place = jnp.zeros_like(apart)
+    place = 0
     at = 0
     for group in phases_of(peers):
         for bit in group:
-            place = place + (((apart // bit) % 2) << at)
+            place = place + (((apart // bit) & 1) << at)
             at += 1
     return place
 
@@ -45,7 +45,17 @@
     return lax.ppermute(x, "sec", [(i, i ^ apart) for i in range(peers)])
 
 
-def mix_kernel(left_ref, vec_ref, mixed_ref):
+def mix_kernel(left_hbm, vec_hbm, env_hbm, mixed_ref, own_ref, left_ref, vec_ref, sems):
+    copies = [
+        pltpu.make_async_copy(left_hbm, left_ref, sems.at[0]),
+        pltpu.make_async_copy(vec_hbm.at[:, 0], vec_ref.at[:, 0], sems.at[1]),
+        pltpu.make_async_copy(vec_hbm.at[:, 1], vec_ref.at[:, 1], sems.at[2]),
+        pltpu.make_async_copy(env_hbm, own_ref, sems.at[3]),
+    ]
+    for copy in copies:
+        copy.start()
+    for copy in copies:
+        copy.wait()
     vecs, secs, width, _ = vec_ref.shape
     terms = left_ref.shape[2] // width
     for a in range(secs):
@@ -56,7 +66,7 @@
                 mixed_ref[a, w, v * width : (v + 1) * width, :] = both[w * width : (w + 1) * width]
 
 
-def close_kernel(at_ref, mixed_ref, env_ref, out_ref, done_ref, sems):
+def close_kernel(peers, dest_ref, slot_ref, mixed_ref, env_ref, out_ref, done_ref, sems):
     secs, terms, tall, wide = mixed_ref.shape
     width = env_ref.shape[1]
     pairs = wide // width
@@ -64,10 +74,15 @@
     lane = lax.broadcasted_iota(jnp.int32, (width, 2 * width), 1)
     low = lane < width
     copies = []
+    me = lax.axis_index("sec")
+
+    def env_at(a, p):
+        return env_ref[place_of(dest_ref[a, p] ^ me, peers) * secs + slot_ref[a, p]]
+
     for a in range(secs):
         for p in range(0, pairs, 2):
-            first = env_ref[at_ref[a, p]]
-            second = env_ref[at_ref[a, p + 1]]
+            first = env_at(a, p)
+            second = env_at(a, p + 1)
             zero = jnp.zeros_like(first)
             top = [jnp.where(low, first, zero), jnp.where(low, pltpu.roll(first, width, 1), zero)]
             bottom = [jnp.where(low, zero, pltpu.roll(second, width, 1)), jnp.where(low, zero, second)]
@@ -91,37 +106,47 @@
     vecs, secs, width, wide = vectors.shape
     pairs = wide // width
     terms = left_env.shape[2] // width
-    me = lax.axis_index("sec")
     dest = target_device.reshape(secs, pairs)
-    at = place_of(dest ^ me, peers) * secs + target_slot
-    mixed = pl.pallas_call(
+    mixed, own = pl.pallas_call(
         mix_kernel,
-        out_shape=jax.ShapeDtypeStruct((secs, terms, vecs * width, wide), jnp.bfloat16),
+        out_shape=(
+            jax.ShapeDtypeStruct((secs, terms, vecs * width, wide), jnp.bfloat16),
+            jax.ShapeDtypeStruct(right_env.shape, right_env.dtype),
+        ),
+        in_specs=[pl.BlockSpec(memory_space=pltpu.HBM)] * 3,
+        scratch_shapes=[
+            pltpu.VMEM(left_env.shape, jnp.bfloat16),
+            pltpu.VMEM(vectors.shape, jnp.bfloat16),
+            pltpu.SemaphoreType.DMA((4,)),
+        ],
+        compiler_params=pltpu.CompilerParams(vmem_limit_bytes=16 * 2**20),
         cost_estimate=pl.CostEstimate(
             flops=2 * vecs * secs * terms * width * width * wide,
             bytes_accessed=6 * vecs * secs * width * wide,
             transcendentals=0,
         ),
-    )(left_env, vectors)
-    env = right_env
+    )(*[pltpu.with_memory_space_constraint(x, pltpu.HBM) for x in (left_env, vectors, right_env)])
+    env, kept = right_env, own
     for group in phases_of(peers):
-        env = jnp.concatenate([env] + [hop(env, s, peers) for s in combos(group)], 0)
+        env = kept = jnp.concatenate([kept] + [hop(env, s, peers) for s in combos(group)], 0)
     return pl.pallas_call(
-        close_kernel,
+        functools.partial(close_kernel, peers),
         out_shape=jax.ShapeDtypeStruct(vectors.shape, jnp.bfloat16),
         in_specs=[
+            pl.BlockSpec(memory_space=pltpu.SMEM),
             pl.BlockSpec(memory_space=pltpu.SMEM),
             pl.BlockSpec(memory_space=pltpu.VMEM),
             pl.BlockSpec(memory_space=pltpu.VMEM),
         ],
         out_specs=pl.BlockSpec(memory_space=pl.ANY),
         scratch_shapes=[pltpu.VMEM(vectors.shape, jnp.bfloat16), pltpu.SemaphoreType.DMA((secs,))],
+        compiler_params=pltpu.CompilerParams(vmem_limit_bytes=16 * 2**20),
         cost_estimate=pl.CostEstimate(
             flops=2 * vecs * secs * terms * width * width * wide,
             bytes_accessed=6 * vecs * secs * width * wide,
             transcendentals=0,
         ),
-    )(at, mixed, env)
+    )(dest, target_slot, mixed, env)
 
 
 def solution(mesh):

time: 22.4 us -> 18.7 us (0.83)
  Pallas kernels: 5.84 us -> 3.88 us
  local copies, waits for them, and re-layouts: 1.74 us -> 0.16 us
  waiting for transfers between devices: 5.55 us -> 6.84 us
  other arithmetic: 1.28 us -> 0 us
    pallas_call x2, Pallas kernels: 5.84 us -> 3.88 us  [the longest x1 2.1 us: body(): pl.pallas_call(functools.partial(close_kernel, peers), out_shape=jax.Shap...]
    unnamed x8, local copies, waits for them, and re-layouts: 1.68 us -> 0.1 us
    ppermute x5, waiting for transfers between devices: 5.55 us -> 6.84 us  [hop(): return lax.ppermute(x, 'sec', [(i, i ^ apart) for i in range(peers)])]
    xor x1 -> x0, other arithmetic: 0.68 us -> none  [body(): at = place_of(dest ^ me, peers) * secs + target_slot]
    add x1 -> x0, other arithmetic: 0.6 us -> none  [body(): at = place_of(dest ^ me, peers) * secs + target_slot]
  transfers between devices with their start and end apart: 5 -> 5, of which waited for: 3 -> 5; matrix products, arithmetic and copies ran while one was open for 10% -> 0% of each run, Pallas kernels for 13% -> 10%
where the time goes in v2:
time: 18.7 us; the launch traced here: 18.6 us
  starting transfers between devices  7.66 us (41%)
  waiting for transfers between devices  6.84 us (37%)
  Pallas kernels  3.88 us (21%)
    ppermute x5, starting transfers between devices, hop(): return lax.ppermute(x, 'sec', [(i, i ^ apart) for i in range(peers)])  7.66 us
    ppermute x5, waiting for transfers between devices, hop(): return lax.ppermute(x, 'sec', [(i, i ^ apart) for i in range(peers)])  6.84 us
    pallas_call x1, Pallas kernels, body(): pl.pallas_call(functools.partial(close_kernel, peers), out_shape=jax.Shap...  2.1 us
    pallas_call x1, Pallas kernels, body(): pl.pallas_call(mix_kernel, out_shape=(jax.ShapeDtypeStruct((secs, terms,...  1.77 us
  transfers between devices with their start and end apart: 5, of which 5 were waited for; matrix products, arithmetic and copies ran while one was open for 0% of the time, Pallas kernels for 10%

profile of v2, /device:TPU:0, one launch (start us, length us, event | category | flops | bytes accessed | tf_op | source)
XLA Modules:
  0.0 18.6 jit_solution(7585036455428797206)
XLA Ops:
  0.0 0.0 copy-start
  0.0 0.0 copy-start.1
  0.0 4.0 %collective-permute-start = (bf16[2,64,128]{2,1,0:T(8,128)(2,1)}, bf16[2,64,128]{2,1,0:T(8,128)(2,1)S(1)}, u32[]{:S(2)}, u32[]{:S(2)}) collective-permute-start(bf16[2,64,128]{2,1,0:T(8,128)(2,1)} %env_hbm.1), channel_id=1, source_target_pairs={{0,8},{1,9},{2,10},{3,11},{4,12},{5,13},{6,14},{7,15},{8,0},{9,1},... | collective-permute-start | bytes 98312 | tf_op jit(solution)/shard_map/ppermute | solution.py:45
  4.0 1.8 %shard_map.55 = (bf16[2,2,192,1024]{3,2,1,0:T(8,128)(2,1)S(1)}, bf16[2,64,128]{2,1,0:T(8,128)(2,1)S(1)}) custom-call(bf16[2,64,128]{2,1,0:T(8,128)(2,1)} %left_hbm.1, bf16[3,2,64,1024]{3,2,1,0:T(8,128)(2,1)} %vec_hbm.1, bf16[2,64,128]{2,1,0:T(8,128)(2,1)} %env_hbm.1), custom_call_target="tpu_custom_call" | custom-call | flops 100663296 | bytes 2359296 | tf_op jit(solution)/shard_map/pallas_call | solution.py:110
  5.8 0.6 %collective-permute-done = bf16[2,64,128]{2,1,0:T(8,128)(2,1)S(1)} collective-permute-done((bf16[2,64,128]{2,1,0:T(8,128)(2,1)}, bf16[2,64,128]{2,1,0:T(8,128)(2,1)S(1)}, u32[]{:S(2)}, u32[]{:S(2)}) %collective-permute-start) | collective-permute-done | bytes 32800 | tf_op jit(solution)/shard_map/ppermute | solution.py:45
  6.5 1.6 %collective-permute-start.1 = (bf16[4,64,128]{2,1,0:T(8,128)(2,1)S(1)}, bf16[4,64,128]{2,1,0:T(8,128)(2,1)S(1)}, u32[]{:S(2)}, u32[]{:S(2)}) collective-permute-start(bf16[4,64,128]{2,1,0:T(8,128)(2,1)S(1)} %get-tuple-element.17), channel_id=1, source_target_pairs={{0,4},{1,5},{2,6},{3,7},{4,0},{5,1},{6,2},{7,3},{8,12},{9,13},{10,... | collective-permute-start | bytes 196616 | tf_op jit(solution)/shard_map/ppermute | solution.py:45
  8.1 1.5 %collective-permute-start.2 = (bf16[4,64,128]{2,1,0:T(8,128)(2,1)S(1)}, bf16[4,64,128]{2,1,0:T(8,128)(2,1)S(1)}, u32[]{:S(2)}, u32[]{:S(2)}) collective-permute-start(bf16[4,64,128]{2,1,0:T(8,128)(2,1)S(1)} %get-tuple-element.17), channel_id=1, source_target_pairs={{0,2},{1,3},{2,0},{3,1},{4,6},{5,7},{6,4},{7,5},{8,10},{9,11},{10,... | collective-permute-start | bytes 196616 | tf_op jit(solution)/shard_map/ppermute | solution.py:45
  9.6 0.4 %collective-permute-start.3 = (bf16[4,64,128]{2,1,0:T(8,128)(2,1)S(1)}, bf16[4,64,128]{2,1,0:T(8,128)(2,1)S(1)}, u32[]{:S(2)}, u32[]{:S(2)}) collective-permute-start(bf16[4,64,128]{2,1,0:T(8,128)(2,1)S(1)} %get-tuple-element.17), channel_id=1, source_target_pairs={{0,6},{1,7},{2,4},{3,5},{4,2},{5,3},{6,0},{7,1},{8,14},{9,15},{10,... | collective-permute-start | bytes 196616 | tf_op jit(solution)/shard_map/ppermute | solution.py:45
  10.1 1.1 %collective-permute-done.1 = bf16[4,64,128]{2,1,0:T(8,128)(2,1)S(1)} collective-permute-done((bf16[4,64,128]{2,1,0:T(8,128)(2,1)S(1)}, bf16[4,64,128]{2,1,0:T(8,128)(2,1)S(1)}, u32[]{:S(2)}, u32[]{:S(2)}) %collective-permute-start.1) | collective-permute-done | bytes 65568 | tf_op jit(solution)/shard_map/ppermute | solution.py:45
  11.2 1.8 %collective-permute-done.2 = bf16[4,64,128]{2,1,0:T(8,128)(2,1)S(1)} collective-permute-done((bf16[4,64,128]{2,1,0:T(8,128)(2,1)S(1)}, bf16[4,64,128]{2,1,0:T(8,128)(2,1)S(1)}, u32[]{:S(2)}, u32[]{:S(2)}) %collective-permute-start.2) | collective-permute-done | bytes 65568 | tf_op jit(solution)/shard_map/ppermute | solution.py:45
  13.0 1.8 %collective-permute-done.3 = bf16[4,64,128]{2,1,0:T(8,128)(2,1)S(1)} collective-permute-done((bf16[4,64,128]{2,1,0:T(8,128)(2,1)S(1)}, bf16[4,64,128]{2,1,0:T(8,128)(2,1)S(1)}, u32[]{:S(2)}, u32[]{:S(2)}) %collective-permute-start.3) | collective-permute-done | bytes 65568 | tf_op jit(solution)/shard_map/ppermute | solution.py:45
  14.8 0.1 collective-permute-start.4
  14.9 1.5 %collective-permute-done.4 = bf16[16,64,128]{2,1,0:T(8,128)(2,1)S(1)} collective-permute-done((bf16[16,64,128]{2,1,0:T(8,128)(2,1)S(1)}, bf16[16,64,128]{2,1,0:T(8,128)(2,1)S(1)}, u32[]{:S(2)}, u32[]{:S(2)}) %collective-permute-start.4) | collective-permute-done | bytes 262176 | tf_op jit(solution)/shard_map/ppermute | solution.py:45
  16.5 0.0 copy-done
  16.5 0.0 copy-done.1
  16.5 2.1 %shard_map.56 = bf16[3,2,64,1024]{3,2,1,0:T(8,128)(2,1)} custom-call(s32[2,16]{1,0:T(2,128)S(1)} %bitcast.1, s32[2,16]{1,0:T(2,128)S(1)} %copy-done.1, bf16[2,2,192,1024]{3,2,1,0:T(8,128)(2,1)S(1)} %get-tuple-element.7.mixed_ref, bf16[32,64,128]{2,1,0:T(8,128)(2,1)S(1)} %constant_dynamic-update-slice_fusion.7.env_ref), custom_call_target="tpu_custom_call" | custom-call | flops 100663296 | bytes 2359296 | tf_op jit(solution)/shard_map/pallas_call | solution.py:132
  (6 shorter events, 0.2 us)
Async XLA Ops:
  0.0 16.5 %copy-start = (s32[2,16,1]{1,2,0:T(1,128)S(1)}, s32[2,16,1]{1,2,0:T(1,128)}, u32[]{:S(2)}) copy-start(s32[2,16,1]{1,2,0:T(1,128)} %param.8) | copy-start | bytes 388
  0.0 16.5 %copy-start.1 = (s32[2,16]{1,0:T(2,128)S(1)}, s32[2,16]{1,0:T(2,128)}, u32[]{:S(2)}) copy-start(s32[2,16]{1,0:T(2,128)} %slot_ref.1) | copy-start | bytes 388
  0.0 6.5 %collective-permute-start = (bf16[2,64,128]{2,1,0:T(8,128)(2,1)}, bf16[2,64,128]{2,1,0:T(8,128)(2,1)S(1)}, u32[]{:S(2)}, u32[]{:S(2)}) collective-permute-start(bf16[2,64,128]{2,1,0:T(8,128)(2,1)} %env_hbm.1), channel_id=1, source_target_pairs={{0,8},{1,9},{2,10},{3,11},{4,12},{5,13},{6,14},{7,15},{8,0},{9,1},... | collective-permute-start | bytes 98312 | tf_op jit(solution)/shard_map/ppermute | solution.py:45
  6.5 4.7 %collective-permute-start.1 = (bf16[4,64,128]{2,1,0:T(8,128)(2,1)S(1)}, bf16[4,64,128]{2,1,0:T(8,128)(2,1)S(1)}, u32[]{:S(2)}, u32[]{:S(2)}) collective-permute-start(bf16[4,64,128]{2,1,0:T(8,128)(2,1)S(1)} %get-tuple-element.17), channel_id=1, source_target_pairs={{0,4},{1,5},{2,6},{3,7},{4,0},{5,1},{6,2},{7,3},{8,12},{9,13},{10,... | collective-permute-start | bytes 196616 | tf_op jit(solution)/shard_map/ppermute | solution.py:45
  8.1 4.9 %collective-permute-start.2 = (bf16[4,64,128]{2,1,0:T(8,128)(2,1)S(1)}, bf16[4,64,128]{2,1,0:T(8,128)(2,1)S(1)}, u32[]{:S(2)}, u32[]{:S(2)}) collective-permute-start(bf16[4,64,128]{2,1,0:T(8,128)(2,1)S(1)} %get-tuple-element.17), channel_id=1, source_target_pairs={{0,2},{1,3},{2,0},{3,1},{4,6},{5,7},{6,4},{7,5},{8,10},{9,11},{10,... | collective-permute-start | bytes 196616 | tf_op jit(solution)/shard_map/ppermute | solution.py:45
  9.6 5.2 %collective-permute-start.3 = (bf16[4,64,128]{2,1,0:T(8,128)(2,1)S(1)}, bf16[4,64,128]{2,1,0:T(8,128)(2,1)S(1)}, u32[]{:S(2)}, u32[]{:S(2)}) collective-permute-start(bf16[4,64,128]{2,1,0:T(8,128)(2,1)S(1)} %get-tuple-element.17), channel_id=1, source_target_pairs={{0,6},{1,7},{2,4},{3,5},{4,2},{5,3},{6,0},{7,1},{8,14},{9,15},{10,... | collective-permute-start | bytes 196616 | tf_op jit(solution)/shard_map/ppermute | solution.py:45
  14.8 1.6 %collective-permute-start.4 = (bf16[16,64,128]{2,1,0:T(8,128)(2,1)S(1)}, bf16[16,64,128]{2,1,0:T(8,128)(2,1)S(1)}, u32[]{:S(2)}, u32[]{:S(2)}) collective-permute-start(bf16[16,64,128]{2,1,0:T(8,128)(2,1)S(1)} %get-tuple-element.9), channel_id=1, source_target_pairs={{0,1},{1,0},{2,3},{3,2},{4,5},{5,4},{6,7},{7,6},{8,9},{9,8},{10,11... | collective-permute-start | bytes 786440 | tf_op jit(solution)/shard_map/ppermute | solution.py:45

commit v3 on v2

--- a/solution.py
+++ b/solution.py
@@ -14,31 +14,45 @@
     while bit > 1:
         bits.append(bit)
         bit //= 2
-    groups = [bits[:1]] if bits else []
-    rest = bits[1:]
-    while rest:
-        groups.append(rest[:2])
-        rest = rest[2:]
-    if peers > 1:
-        groups.append([1])
+    groups = [[(bits[0], bits[0])]] if bits else []
+    for i in range(1, len(bits), 2):
+        if i + 1 == len(bits):
+            groups.append([(bits[i], bits[i])])
+        else:
+            high, low = bits[i], bits[i + 1]
+            groups.append([(high | low, high), (low, high | low)])
     return groups
 
 
 def combos(group):
     sums = [0]
-    for bit in group:
-        sums = sums + [s ^ bit for s in sums]
+    for mask, _ in group:
+        sums = sums + [s ^ mask for s in sums]
     return sums[1:]
+
+
+def parity(x, test):
+    total, bit = 0, 1
+    while bit <= test:
+        if test & bit:
+            total = total ^ ((x // bit) & 1)
+        bit *= 2
+    return total
 
 
 def place_of(apart, peers):
     place = 0
     at = 0
+    flips = apart & 1
     for group in phases_of(peers):
-        for bit in group:
-            place = place + (((apart // bit) & 1) << at)
+        some = 0
+        for mask, test in group:
+            own = parity(apart, test)
+            place = place + (own << at)
+            some = some | own
             at += 1
-    return place
+        flips = flips ^ some
+    return place + (flips << at)
 
 
 def hop(x, apart, peers):
@@ -128,7 +142,9 @@
     )(*[pltpu.with_memory_space_constraint(x, pltpu.HBM) for x in (left_env, vectors, right_env)])
     env, kept = right_env, own
     for group in phases_of(peers):
-        env = kept = jnp.concatenate([kept] + [hop(env, s, peers) for s in combos(group)], 0)
+        env = kept = jnp.concatenate([kept] + [hop(env, s | 1, peers) for s in combos(group)], 0)
+    if peers > 1:
+        env = jnp.concatenate([env, hop(env, 1, peers)], 0)
     return pl.pallas_call(
         functools.partial(close_kernel, peers),
         out_shape=jax.ShapeDtypeStruct(vectors.shape, jnp.bfloat16),

time: 18.7 us -> 16.9 us (0.904)
  waiting for transfers between devices: 6.84 us -> 5.57 us
  starting transfers between devices: 7.66 us -> 7.06 us
    ppermute x5, waiting for transfers between devices: 6.84 us -> 5.57 us  [hop(): return lax.ppermute(x, 'sec', [(i, i ^ apart) for i in range(peers)])]
    ppermute x5, starting transfers between devices: 7.66 us -> 7.06 us  [hop(): return lax.ppermute(x, 'sec', [(i, i ^ apart) for i in range(peers)])]
  transfers between devices with their start and end apart: 5 -> 5, of which waited for: 5 -> 5; matrix products, arithmetic and copies ran while one was open for 0% -> 0% of each run, Pallas kernels for 10% -> 11%
where the time goes in v3:
time: 16.9 us; the launch traced here: 16.7 us
  starting transfers between devices  7.06 us (42%)
  waiting for transfers between devices  5.57 us (33%)
  Pallas kernels  3.88 us (23%)
    ppermute x5, starting transfers between devices, hop(): return lax.ppermute(x, 'sec', [(i, i ^ apart) for i in range(peers)])  7.06 us
    ppermute x5, waiting for transfers between devices, hop(): return lax.ppermute(x, 'sec', [(i, i ^ apart) for i in range(peers)])  5.57 us
    pallas_call x1, Pallas kernels, body(): pl.pallas_call(functools.partial(close_kernel, peers), out_shape=jax.Shap...  2.12 us
    pallas_call x1, Pallas kernels, body(): pl.pallas_call(mix_kernel, out_shape=(jax.ShapeDtypeStruct((secs, terms,...  1.76 us
  transfers between devices with their start and end apart: 5, of which 5 were waited for; matrix products, arithmetic and copies ran while one was open for 0% of the time, Pallas kernels for 11%

profile of v3, /device:TPU:0, one launch (start us, length us, event | category | flops | bytes accessed | tf_op | source)
XLA Modules:
  0.0 16.7 jit_solution(4397608922875370221)
XLA Ops:
  0.0 0.0 copy-start
  0.0 0.0 copy-start.1
  0.0 3.5 %collective-permute-start = (bf16[2,64,128]{2,1,0:T(8,128)(2,1)}, bf16[2,64,128]{2,1,0:T(8,128)(2,1)S(1)}, u32[]{:S(2)}, u32[]{:S(2)}) collective-permute-start(bf16[2,64,128]{2,1,0:T(8,128)(2,1)} %env_hbm.1), channel_id=1, source_target_pairs={{0,9},{1,8},{2,11},{3,10},{4,13},{5,12},{6,15},{7,14},{8,1},{9,0},... | collective-permute-start | bytes 98312 | tf_op jit(solution)/shard_map/ppermute | solution.py:59
  3.5 1.8 %shard_map.55 = (bf16[2,2,192,1024]{3,2,1,0:T(8,128)(2,1)S(1)}, bf16[2,64,128]{2,1,0:T(8,128)(2,1)S(1)}) custom-call(bf16[2,64,128]{2,1,0:T(8,128)(2,1)} %left_hbm.1, bf16[3,2,64,1024]{3,2,1,0:T(8,128)(2,1)} %vec_hbm.1, bf16[2,64,128]{2,1,0:T(8,128)(2,1)} %env_hbm.1), custom_call_target="tpu_custom_call" | custom-call | flops 100663296 | bytes 2359296 | tf_op jit(solution)/shard_map/pallas_call | solution.py:124
  5.3 0.3 %collective-permute-done = bf16[2,64,128]{2,1,0:T(8,128)(2,1)S(1)} collective-permute-done((bf16[2,64,128]{2,1,0:T(8,128)(2,1)}, bf16[2,64,128]{2,1,0:T(8,128)(2,1)S(1)}, u32[]{:S(2)}, u32[]{:S(2)}) %collective-permute-start) | collective-permute-done | bytes 32800 | tf_op jit(solution)/shard_map/ppermute | solution.py:59
  5.6 2.7 %collective-permute-start.1 = (bf16[4,64,128]{2,1,0:T(8,128)(2,1)S(1)}, bf16[4,64,128]{2,1,0:T(8,128)(2,1)S(1)}, u32[]{:S(2)}, u32[]{:S(2)}) collective-permute-start(bf16[4,64,128]{2,1,0:T(8,128)(2,1)S(1)} %get-tuple-element.17), channel_id=1, source_target_pairs={{0,7},{1,6},{2,5},{3,4},{4,3},{5,2},{6,1},{7,0},{8,15},{9,14},{10,... | collective-permute-start | bytes 196616 | tf_op jit(solution)/shard_map/ppermute | solution.py:59
  8.3 0.5 %collective-permute-start.2 = (bf16[4,64,128]{2,1,0:T(8,128)(2,1)S(1)}, bf16[4,64,128]{2,1,0:T(8,128)(2,1)S(1)}, u32[]{:S(2)}, u32[]{:S(2)}) collective-permute-start(bf16[4,64,128]{2,1,0:T(8,128)(2,1)S(1)} %get-tuple-element.17), channel_id=1, source_target_pairs={{0,3},{1,2},{2,1},{3,0},{4,7},{5,6},{6,5},{7,4},{8,11},{9,10},{10,... | collective-permute-start | bytes 196616 | tf_op jit(solution)/shard_map/ppermute | solution.py:59
  8.9 0.1 collective-permute-start.3
  9.0 1.9 %collective-permute-done.1 = bf16[4,64,128]{2,1,0:T(8,128)(2,1)S(1)} collective-permute-done((bf16[4,64,128]{2,1,0:T(8,128)(2,1)S(1)}, bf16[4,64,128]{2,1,0:T(8,128)(2,1)S(1)}, u32[]{:S(2)}, u32[]{:S(2)}) %collective-permute-start.1) | collective-permute-done | bytes 65568 | tf_op jit(solution)/shard_map/ppermute | solution.py:59
  10.9 1.4 %collective-permute-done.2 = bf16[4,64,128]{2,1,0:T(8,128)(2,1)S(1)} collective-permute-done((bf16[4,64,128]{2,1,0:T(8,128)(2,1)S(1)}, bf16[4,64,128]{2,1,0:T(8,128)(2,1)S(1)}, u32[]{:S(2)}, u32[]{:S(2)}) %collective-permute-start.2) | collective-permute-done | bytes 65568 | tf_op jit(solution)/shard_map/ppermute | solution.py:59
  12.3 0.6 %collective-permute-done.3 = bf16[4,64,128]{2,1,0:T(8,128)(2,1)S(1)} collective-permute-done((bf16[4,64,128]{2,1,0:T(8,128)(2,1)S(1)}, bf16[4,64,128]{2,1,0:T(8,128)(2,1)S(1)}, u32[]{:S(2)}, u32[]{:S(2)}) %collective-permute-start.3) | collective-permute-done | bytes 65568 | tf_op jit(solution)/shard_map/ppermute | solution.py:59
  13.0 0.2 %collective-permute-start.4 = (bf16[16,64,128]{2,1,0:T(8,128)(2,1)S(1)}, bf16[16,64,128]{2,1,0:T(8,128)(2,1)S(1)}, u32[]{:S(2)}, u32[]{:S(2)}) collective-permute-start(bf16[16,64,128]{2,1,0:T(8,128)(2,1)S(1)} %get-tuple-element.9), channel_id=1, source_target_pairs={{0,1},{1,0},{2,3},{3,2},{4,5},{5,4},{6,7},{7,6},{8,9},{9,8},{10,11... | collective-permute-start | bytes 786440 | tf_op jit(solution)/shard_map/ppermute | solution.py:59
  13.2 1.4 %collective-permute-done.4 = bf16[16,64,128]{2,1,0:T(8,128)(2,1)S(1)} collective-permute-done((bf16[16,64,128]{2,1,0:T(8,128)(2,1)S(1)}, bf16[16,64,128]{2,1,0:T(8,128)(2,1)S(1)}, u32[]{:S(2)}, u32[]{:S(2)}) %collective-permute-start.4) | collective-permute-done | bytes 262176 | tf_op jit(solution)/shard_map/ppermute | solution.py:59
  14.6 0.0 copy-done
  14.6 0.0 copy-done.1
  14.6 2.1 %shard_map.56 = bf16[3,2,64,1024]{3,2,1,0:T(8,128)(2,1)} custom-call(s32[2,16]{1,0:T(2,128)S(1)} %bitcast.1, s32[2,16]{1,0:T(2,128)S(1)} %copy-done.1, bf16[2,2,192,1024]{3,2,1,0:T(8,128)(2,1)S(1)} %get-tuple-element.7.mixed_ref, bf16[32,64,128]{2,1,0:T(8,128)(2,1)S(1)} %constant_dynamic-update-slice_fusion.7.env_ref), custom_call_target="tpu_custom_call" | custom-call | flops 100663296 | bytes 2359296 | tf_op jit(solution)/shard_map/pallas_call | solution.py:148
  (6 shorter events, 0.2 us)
Async XLA Ops:
  0.0 14.6 %copy-start = (s32[2,16,1]{1,2,0:T(1,128)S(1)}, s32[2,16,1]{1,2,0:T(1,128)}, u32[]{:S(2)}) copy-start(s32[2,16,1]{1,2,0:T(1,128)} %param.8) | copy-start | bytes 388
  0.0 14.6 %copy-start.1 = (s32[2,16]{1,0:T(2,128)S(1)}, s32[2,16]{1,0:T(2,128)}, u32[]{:S(2)}) copy-start(s32[2,16]{1,0:T(2,128)} %slot_ref.1) | copy-start | bytes 388
  0.0 5.6 %collective-permute-start = (bf16[2,64,128]{2,1,0:T(8,128)(2,1)}, bf16[2,64,128]{2,1,0:T(8,128)(2,1)S(1)}, u32[]{:S(2)}, u32[]{:S(2)}) collective-permute-start(bf16[2,64,128]{2,1,0:T(8,128)(2,1)} %env_hbm.1), channel_id=1, source_target_pairs={{0,9},{1,8},{2,11},{3,10},{4,13},{5,12},{6,15},{7,14},{8,1},{9,0},... | collective-permute-start | bytes 98312 | tf_op jit(solution)/shard_map/ppermute | solution.py:59
  5.6 5.3 %collective-permute-start.1 = (bf16[4,64,128]{2,1,0:T(8,128)(2,1)S(1)}, bf16[4,64,128]{2,1,0:T(8,128)(2,1)S(1)}, u32[]{:S(2)}, u32[]{:S(2)}) collective-permute-start(bf16[4,64,128]{2,1,0:T(8,128)(2,1)S(1)} %get-tuple-element.17), channel_id=1, source_target_pairs={{0,7},{1,6},{2,5},{3,4},{4,3},{5,2},{6,1},{7,0},{8,15},{9,14},{10,... | collective-permute-start | bytes 196616 | tf_op jit(solution)/shard_map/ppermute | solution.py:59
  8.3 3.9 %collective-permute-start.2 = (bf16[4,64,128]{2,1,0:T(8,128)(2,1)S(1)}, bf16[4,64,128]{2,1,0:T(8,128)(2,1)S(1)}, u32[]{:S(2)}, u32[]{:S(2)}) collective-permute-start(bf16[4,64,128]{2,1,0:T(8,128)(2,1)S(1)} %get-tuple-element.17), channel_id=1, source_target_pairs={{0,3},{1,2},{2,1},{3,0},{4,7},{5,6},{6,5},{7,4},{8,11},{9,10},{10,... | collective-permute-start | bytes 196616 | tf_op jit(solution)/shard_map/ppermute | solution.py:59
  8.9 4.1 %collective-permute-start.3 = (bf16[4,64,128]{2,1,0:T(8,128)(2,1)S(1)}, bf16[4,64,128]{2,1,0:T(8,128)(2,1)S(1)}, u32[]{:S(2)}, u32[]{:S(2)}) collective-permute-start(bf16[4,64,128]{2,1,0:T(8,128)(2,1)S(1)} %get-tuple-element.17), channel_id=1, source_target_pairs={{0,5},{1,4},{2,7},{3,6},{4,1},{5,0},{6,3},{7,2},{8,13},{9,12},{10,... | collective-permute-start | bytes 196616 | tf_op jit(solution)/shard_map/ppermute | solution.py:59
  13.0 1.6 %collective-permute-start.4 = (bf16[16,64,128]{2,1,0:T(8,128)(2,1)S(1)}, bf16[16,64,128]{2,1,0:T(8,128)(2,1)S(1)}, u32[]{:S(2)}, u32[]{:S(2)}) collective-permute-start(bf16[16,64,128]{2,1,0:T(8,128)(2,1)S(1)} %get-tuple-element.9), channel_id=1, source_target_pairs={{0,1},{1,0},{2,3},{3,2},{4,5},{5,4},{6,7},{7,6},{8,9},{9,8},{10,11... | collective-permute-start | bytes 786440 | tf_op jit(solution)/shard_map/ppermute | solution.py:59

commit v4 on v3

--- a/solution.py
+++ b/solution.py
@@ -59,50 +59,61 @@
     return lax.ppermute(x, "sec", [(i, i ^ apart) for i in range(peers)])
 
 
-def mix_kernel(left_hbm, vec_hbm, env_hbm, mixed_ref, own_ref, left_ref, vec_ref, sems):
+def mix_kernel(peers, left_hbm, vec_hbm, env_hbm, dest_hbm, slot_hbm, mixed_ref, own_ref, at_ref, left_ref, vec_ref, dest_ref, slot_ref, sems):
     copies = [
         pltpu.make_async_copy(left_hbm, left_ref, sems.at[0]),
         pltpu.make_async_copy(vec_hbm.at[:, 0], vec_ref.at[:, 0], sems.at[1]),
         pltpu.make_async_copy(vec_hbm.at[:, 1], vec_ref.at[:, 1], sems.at[2]),
         pltpu.make_async_copy(env_hbm, own_ref, sems.at[3]),
+        pltpu.make_async_copy(dest_hbm, dest_ref, sems.at[4]),
+        pltpu.make_async_copy(slot_hbm, slot_ref, sems.at[5]),
     ]
     for copy in copies:
         copy.start()
     for copy in copies:
         copy.wait()
-    vecs, secs, width, _ = vec_ref.shape
-    terms = left_ref.shape[2] // width
+    me = lax.axis_index("sec")
+    at_ref[...] = place_of(dest_ref[...] ^ me, peers) * vec_ref.shape[1] + slot_ref[...]
+    vecs, secs, width, wide = vec_ref.shape
+    low = lax.broadcasted_iota(jnp.int32, (width, wide), 1) % (2 * width) < width
+
+    def turn(x):
+        parts = [
+            pltpu.roll(x[:, c : c + 2 * width], width, 1) for c in range(0, wide, 2 * width)
+        ]
+        return jnp.concatenate(parts, 1)
+
     for a in range(secs):
         turned = left_ref[a].T
         for v in range(vecs):
             both = jnp.dot(turned, vec_ref[v, a], preferred_element_type=jnp.float32).astype(jnp.bfloat16)
-            for w in range(terms):
-                mixed_ref[a, w, v * width : (v + 1) * width, :] = both[w * width : (w + 1) * width]
+            first, second = both[:width], both[width:]
+            mixed_ref[a, 0, v * width : (v + 1) * width, :] = jnp.where(low, first, turn(second))
+            mixed_ref[a, 1, v * width : (v + 1) * width, :] = jnp.where(low, turn(first), second)
 
 
-def close_kernel(peers, dest_ref, slot_ref, mixed_ref, env_ref, out_ref, done_ref, sems):
+def close_kernel(at_ref, mixed_ref, env_ref, out_ref, done_ref, sems):
     secs, terms, tall, wide = mixed_ref.shape
     width = env_ref.shape[1]
     pairs = wide // width
     vecs = tall // width
-    lane = lax.broadcasted_iota(jnp.int32, (width, 2 * width), 1)
-    low = lane < width
     copies = []
-    me = lax.axis_index("sec")
+
+    where = at_ref[...]
 
     def env_at(a, p):
-        return env_ref[place_of(dest_ref[a, p] ^ me, peers) * secs + slot_ref[a, p]]
+        return env_ref[where[a, p]]
 
     for a in range(secs):
         for p in range(0, pairs, 2):
             first = env_at(a, p)
             second = env_at(a, p + 1)
             zero = jnp.zeros_like(first)
-            top = [jnp.where(low, first, zero), jnp.where(low, pltpu.roll(first, width, 1), zero)]
-            bottom = [jnp.where(low, zero, pltpu.roll(second, width, 1)), jnp.where(low, zero, second)]
-            weights = jnp.concatenate([jnp.concatenate(top, 1), jnp.concatenate(bottom, 1)], 0)
+            top = jnp.concatenate([first, zero], 1)
+            bottom = jnp.concatenate([zero, second], 1)
+            weights = jnp.concatenate([top, bottom], 0)
             cols = slice(p * width, (p + 2) * width)
-            rows = jnp.concatenate([mixed_ref[a, w, :, cols] for w in range(terms)], 1)
+            rows = jnp.concatenate([mixed_ref[a, w, :, cols] for w in range(2)], 1)
             block = lax.dot_general(
                 rows, weights, (((1,), (1,)), ((), ())), preferred_element_type=jnp.float32
             ).astype(jnp.bfloat16)
@@ -121,17 +132,20 @@
     pairs = wide // width
     terms = left_env.shape[2] // width
     dest = target_device.reshape(secs, pairs)
-    mixed, own = pl.pallas_call(
-        mix_kernel,
+    mixed, own, at = pl.pallas_call(
+        functools.partial(mix_kernel, peers),
         out_shape=(
             jax.ShapeDtypeStruct((secs, terms, vecs * width, wide), jnp.bfloat16),
             jax.ShapeDtypeStruct(right_env.shape, right_env.dtype),
+            jax.ShapeDtypeStruct(target_slot.shape, jnp.int32),
         ),
-        in_specs=[pl.BlockSpec(memory_space=pltpu.HBM)] * 3,
+        in_specs=[pl.BlockSpec(memory_space=pltpu.HBM)] * 5,
         scratch_shapes=[
             pltpu.VMEM(left_env.shape, jnp.bfloat16),
             pltpu.VMEM(vectors.shape, jnp.bfloat16),
-            pltpu.SemaphoreType.DMA((4,)),
+            pltpu.VMEM(dest.shape, jnp.int32),
+            pltpu.VMEM(target_slot.shape, jnp.int32),
+            pltpu.SemaphoreType.DMA((6,)),
         ],
         compiler_params=pltpu.CompilerParams(vmem_limit_bytes=16 * 2**20),
         cost_estimate=pl.CostEstimate(
@@ -139,18 +153,17 @@
             bytes_accessed=6 * vecs * secs * width * wide,
             transcendentals=0,
         ),
-    )(*[pltpu.with_memory_space_constraint(x, pltpu.HBM) for x in (left_env, vectors, right_env)])
+    )(*[pltpu.with_memory_space_constraint(x, pltpu.HBM) for x in (left_env, vectors, right_env, dest, target_slot)])
     env, kept = right_env, own
     for group in phases_of(peers):
         env = kept = jnp.concatenate([kept] + [hop(env, s | 1, peers) for s in combos(group)], 0)
     if peers > 1:
         env = jnp.concatenate([env, hop(env, 1, peers)], 0)
     return pl.pallas_call(
-        functools.partial(close_kernel, peers),
+        close_kernel,
         out_shape=jax.ShapeDtypeStruct(vectors.shape, jnp.bfloat16),
         in_specs=[
-            pl.BlockSpec(memory_space=pltpu.SMEM),
-            pl.BlockSpec(memory_space=pltpu.SMEM),
+            pl.BlockSpec(memory_space=pltpu.VMEM),
             pl.BlockSpec(memory_space=pltpu.VMEM),
             pl.BlockSpec(memory_space=pltpu.VMEM),
         ],
@@ -162,7 +175,7 @@
             bytes_accessed=6 * vecs * secs * width * wide,
             transcendentals=0,
         ),
-    )(dest, target_slot, mixed, env)
+    )(at, mixed, env)
 
 
 def solution(mesh):

time: 16.9 us -> 16.2 us (0.959)
  Pallas kernels: 3.88 us -> 3.35 us
    pallas_call x2, Pallas kernels: 3.88 us -> 3.35 us  [the longest x1 1.87 us: body(): pl.pallas_call(functools.partial(mix_kernel, peers), out_shape=(jax.Shape...]
  transfers between devices with their start and end apart: 5 -> 5, of which waited for: 5 -> 5; matrix products, arithmetic and copies ran while one was open for 0% -> 0% of each run, Pallas kernels for 11% -> 12%
where the time goes in v4:
time: 16.2 us; the launch traced here: 16.1 us
  starting transfers between devices  7.1 us (44%)
  waiting for transfers between devices  5.42 us (33%)
  Pallas kernels  3.35 us (21%)
    ppermute x5, starting transfers between devices, hop(): return lax.ppermute(x, 'sec', [(i, i ^ apart) for i in range(peers)])  7.1 us
    ppermute x5, waiting for transfers between devices, hop(): return lax.ppermute(x, 'sec', [(i, i ^ apart) for i in range(peers)])  5.42 us
    pallas_call x1, Pallas kernels, body(): pl.pallas_call(functools.partial(mix_kernel, peers), out_shape=(jax.Shape...  1.87 us
    pallas_call x1, Pallas kernels, body(): pl.pallas_call(close_kernel, out_shape=jax.ShapeDtypeStruct(vectors.shape...  1.48 us
  transfers between devices with their start and end apart: 5, of which 5 were waited for; matrix products, arithmetic and copies ran while one was open for 0% of the time, Pallas kernels for 12%

profile of v4, /device:TPU:0, one launch (start us, length us, event | category | flops | bytes accessed | tf_op | source)
XLA Modules:
  0.0 16.1 jit_solution(7296463500893217654)
XLA Ops:
  0.0 3.5 %collective-permute-start = (bf16[2,64,128]{2,1,0:T(8,128)(2,1)}, bf16[2,64,128]{2,1,0:T(8,128)(2,1)S(1)}, u32[]{:S(2)}, u32[]{:S(2)}) collective-permute-start(bf16[2,64,128]{2,1,0:T(8,128)(2,1)} %env_hbm.1), channel_id=1, source_target_pairs={{0,9},{1,8},{2,11},{3,10},{4,13},{5,12},{6,15},{7,14},{8,1},{9,0},... | collective-permute-start | bytes 98312 | tf_op jit(solution)/shard_map/ppermute | solution.py:59
  3.5 1.9 %shard_map.55 = (bf16[2,2,192,1024]{3,2,1,0:T(8,128)(2,1)S(1)}, bf16[2,64,128]{2,1,0:T(8,128)(2,1)S(1)}, s32[2,16]{1,0:T(2,128)S(1)}) custom-call(bf16[2,64,128]{2,1,0:T(8,128)(2,1)} %left_hbm.1, bf16[3,2,64,1024]{3,2,1,0:T(8,128)(2,1)} %vec_hbm.1, bf16[2,64,128]{2,1,0:T(8,128)(2,1)} %env_hbm.1, s32[2,16]{1,0:T(2,128)} %bitcast.1, s32[2,16]{1,0:T(2,128)} %slot_hbm.1), custom_call_target="tpu_custom_call" | custom-call | flops 100663296 | bytes 2359296 | tf_op jit(solution)/shard_map/pallas_call | solution.py:135
  5.4 0.2 %collective-permute-done = bf16[2,64,128]{2,1,0:T(8,128)(2,1)S(1)} collective-permute-done((bf16[2,64,128]{2,1,0:T(8,128)(2,1)}, bf16[2,64,128]{2,1,0:T(8,128)(2,1)S(1)}, u32[]{:S(2)}, u32[]{:S(2)}) %collective-permute-start) | collective-permute-done | bytes 32800 | tf_op jit(solution)/shard_map/ppermute | solution.py:59
  5.6 2.7 %collective-permute-start.1 = (bf16[4,64,128]{2,1,0:T(8,128)(2,1)S(1)}, bf16[4,64,128]{2,1,0:T(8,128)(2,1)S(1)}, u32[]{:S(2)}, u32[]{:S(2)}) collective-permute-start(bf16[4,64,128]{2,1,0:T(8,128)(2,1)S(1)} %get-tuple-element.19), channel_id=1, source_target_pairs={{0,7},{1,6},{2,5},{3,4},{4,3},{5,2},{6,1},{7,0},{8,15},{9,14},{10,... | collective-permute-start | bytes 196616 | tf_op jit(solution)/shard_map/ppermute | solution.py:59
  8.3 0.5 %collective-permute-start.2 = (bf16[4,64,128]{2,1,0:T(8,128)(2,1)S(1)}, bf16[4,64,128]{2,1,0:T(8,128)(2,1)S(1)}, u32[]{:S(2)}, u32[]{:S(2)}) collective-permute-start(bf16[4,64,128]{2,1,0:T(8,128)(2,1)S(1)} %get-tuple-element.19), channel_id=1, source_target_pairs={{0,3},{1,2},{2,1},{3,0},{4,7},{5,6},{6,5},{7,4},{8,11},{9,10},{10,... | collective-permute-start | bytes 196616 | tf_op jit(solution)/shard_map/ppermute | solution.py:59
  8.9 0.1 collective-permute-start.3
  9.0 1.8 %collective-permute-done.1 = bf16[4,64,128]{2,1,0:T(8,128)(2,1)S(1)} collective-permute-done((bf16[4,64,128]{2,1,0:T(8,128)(2,1)S(1)}, bf16[4,64,128]{2,1,0:T(8,128)(2,1)S(1)}, u32[]{:S(2)}, u32[]{:S(2)}) %collective-permute-start.1) | collective-permute-done | bytes 65568 | tf_op jit(solution)/shard_map/ppermute | solution.py:59
  10.9 1.4 %collective-permute-done.2 = bf16[4,64,128]{2,1,0:T(8,128)(2,1)S(1)} collective-permute-done((bf16[4,64,128]{2,1,0:T(8,128)(2,1)S(1)}, bf16[4,64,128]{2,1,0:T(8,128)(2,1)S(1)}, u32[]{:S(2)}, u32[]{:S(2)}) %collective-permute-start.2) | collective-permute-done | bytes 65568 | tf_op jit(solution)/shard_map/ppermute | solution.py:59
  12.3 0.6 %collective-permute-done.3 = bf16[4,64,128]{2,1,0:T(8,128)(2,1)S(1)} collective-permute-done((bf16[4,64,128]{2,1,0:T(8,128)(2,1)S(1)}, bf16[4,64,128]{2,1,0:T(8,128)(2,1)S(1)}, u32[]{:S(2)}, u32[]{:S(2)}) %collective-permute-start.3) | collective-permute-done | bytes 65568 | tf_op jit(solution)/shard_map/ppermute | solution.py:59
  12.9 0.2 %collective-permute-start.4 = (bf16[16,64,128]{2,1,0:T(8,128)(2,1)S(1)}, bf16[16,64,128]{2,1,0:T(8,128)(2,1)S(1)}, u32[]{:S(2)}, u32[]{:S(2)}) collective-permute-start(bf16[16,64,128]{2,1,0:T(8,128)(2,1)S(1)} %get-tuple-element.11), channel_id=1, source_target_pairs={{0,1},{1,0},{2,3},{3,2},{4,5},{5,4},{6,7},{7,6},{8,9},{9,8},{10,11... | collective-permute-start | bytes 786440 | tf_op jit(solution)/shard_map/ppermute | solution.py:59
  13.2 1.4 %collective-permute-done.4 = bf16[16,64,128]{2,1,0:T(8,128)(2,1)S(1)} collective-permute-done((bf16[16,64,128]{2,1,0:T(8,128)(2,1)S(1)}, bf16[16,64,128]{2,1,0:T(8,128)(2,1)S(1)}, u32[]{:S(2)}, u32[]{:S(2)}) %collective-permute-start.4) | collective-permute-done | bytes 262176 | tf_op jit(solution)/shard_map/ppermute | solution.py:59
  14.6 1.5 %shard_map.56 = bf16[3,2,64,1024]{3,2,1,0:T(8,128)(2,1)} custom-call(s32[2,16]{1,0:T(2,128)S(1)} %get-tuple-element.8.at_ref, bf16[2,2,192,1024]{3,2,1,0:T(8,128)(2,1)S(1)} %get-tuple-element.9.mixed_ref, bf16[32,64,128]{2,1,0:T(8,128)(2,1)S(1)} %constant_dynamic-update-slice_fusion.7.env_ref), custom_call_target="tpu_custom_call" | custom-call | flops 100663296 | bytes 2359296 | tf_op jit(solution)/shard_map/pallas_call | solution.py:162
  (6 shorter events, 0.2 us)
Async XLA Ops:
  0.0 5.6 %collective-permute-start = (bf16[2,64,128]{2,1,0:T(8,128)(2,1)}, bf16[2,64,128]{2,1,0:T(8,128)(2,1)S(1)}, u32[]{:S(2)}, u32[]{:S(2)}) collective-permute-start(bf16[2,64,128]{2,1,0:T(8,128)(2,1)} %env_hbm.1), channel_id=1, source_target_pairs={{0,9},{1,8},{2,11},{3,10},{4,13},{5,12},{6,15},{7,14},{8,1},{9,0},... | collective-permute-start | bytes 98312 | tf_op jit(solution)/shard_map/ppermute | solution.py:59
  5.6 5.3 %collective-permute-start.1 = (bf16[4,64,128]{2,1,0:T(8,128)(2,1)S(1)}, bf16[4,64,128]{2,1,0:T(8,128)(2,1)S(1)}, u32[]{:S(2)}, u32[]{:S(2)}) collective-permute-start(bf16[4,64,128]{2,1,0:T(8,128)(2,1)S(1)} %get-tuple-element.19), channel_id=1, source_target_pairs={{0,7},{1,6},{2,5},{3,4},{4,3},{5,2},{6,1},{7,0},{8,15},{9,14},{10,... | collective-permute-start | bytes 196616 | tf_op jit(solution)/shard_map/ppermute | solution.py:59
  8.3 3.9 %collective-permute-start.2 = (bf16[4,64,128]{2,1,0:T(8,128)(2,1)S(1)}, bf16[4,64,128]{2,1,0:T(8,128)(2,1)S(1)}, u32[]{:S(2)}, u32[]{:S(2)}) collective-permute-start(bf16[4,64,128]{2,1,0:T(8,128)(2,1)S(1)} %get-tuple-element.19), channel_id=1, source_target_pairs={{0,3},{1,2},{2,1},{3,0},{4,7},{5,6},{6,5},{7,4},{8,11},{9,10},{10,... | collective-permute-start | bytes 196616 | tf_op jit(solution)/shard_map/ppermute | solution.py:59
  8.9 4.1 %collective-permute-start.3 = (bf16[4,64,128]{2,1,0:T(8,128)(2,1)S(1)}, bf16[4,64,128]{2,1,0:T(8,128)(2,1)S(1)}, u32[]{:S(2)}, u32[]{:S(2)}) collective-permute-start(bf16[4,64,128]{2,1,0:T(8,128)(2,1)S(1)} %get-tuple-element.19), channel_id=1, source_target_pairs={{0,5},{1,4},{2,7},{3,6},{4,1},{5,0},{6,3},{7,2},{8,13},{9,12},{10,... | collective-permute-start | bytes 196616 | tf_op jit(solution)/shard_map/ppermute | solution.py:59
  12.9 1.6 %collective-permute-start.4 = (bf16[16,64,128]{2,1,0:T(8,128)(2,1)S(1)}, bf16[16,64,128]{2,1,0:T(8,128)(2,1)S(1)}, u32[]{:S(2)}, u32[]{:S(2)}) collective-permute-start(bf16[16,64,128]{2,1,0:T(8,128)(2,1)S(1)} %get-tuple-element.11), channel_id=1, source_target_pairs={{0,1},{1,0},{2,3},{3,2},{4,5},{5,4},{6,7},{7,6},{8,9},{9,8},{10,11... | collective-permute-start | bytes 786440 | tf_op jit(solution)/shard_map/ppermute | solution.py:59

commit v5 on v4

--- a/solution.py
+++ b/solution.py
@@ -20,7 +20,7 @@
             groups.append([(bits[i], bits[i])])
         else:
             high, low = bits[i], bits[i + 1]
-            groups.append([(high | low, high), (low, high | low)])
+            groups.append([(high, high | low), (high | low, low)])
     return groups
 
 
@@ -44,13 +44,15 @@
     place = 0
     at = 0
     flips = apart & 1
-    for group in phases_of(peers):
+    for turn, group in enumerate(phases_of(peers)):
         some = 0
         for mask, test in group:
             own = parity(apart, test)
             place = place + (own << at)
             some = some | own
             at += 1
+        if turn > 0:
+            place = place ^ (1 << (at - 1))
         flips = flips ^ some
     return place + (flips << at)
 
@@ -59,17 +61,17 @@
     return lax.ppermute(x, "sec", [(i, i ^ apart) for i in range(peers)])
 
 
-def mix_kernel(peers, left_hbm, vec_hbm, env_hbm, dest_hbm, slot_hbm, mixed_ref, own_ref, at_ref, left_ref, vec_ref, dest_ref, slot_ref, sems):
+def mix_kernel(peers, left_hbm, vec_hbm, dest_hbm, slot_hbm, env_ref, mixed_ref, kept_ref, at_ref, left_ref, vec_ref, dest_ref, slot_ref, sems):
     copies = [
         pltpu.make_async_copy(left_hbm, left_ref, sems.at[0]),
         pltpu.make_async_copy(vec_hbm.at[:, 0], vec_ref.at[:, 0], sems.at[1]),
         pltpu.make_async_copy(vec_hbm.at[:, 1], vec_ref.at[:, 1], sems.at[2]),
-        pltpu.make_async_copy(env_hbm, own_ref, sems.at[3]),
-        pltpu.make_async_copy(dest_hbm, dest_ref, sems.at[4]),
-        pltpu.make_async_copy(slot_hbm, slot_ref, sems.at[5]),
+        pltpu.make_async_copy(dest_hbm, dest_ref, sems.at[3]),
+        pltpu.make_async_copy(slot_hbm, slot_ref, sems.at[4]),
     ]
     for copy in copies:
         copy.start()
+    kept_ref[...] = env_ref[...]
     for copy in copies:
         copy.wait()
     me = lax.axis_index("sec")
@@ -132,20 +134,24 @@
     pairs = wide // width
     terms = left_env.shape[2] // width
     dest = target_device.reshape(secs, pairs)
-    mixed, own, at = pl.pallas_call(
+    groups = phases_of(peers)
+    env = right_env
+    for group in groups[:1]:
+        env = jnp.concatenate([env] + [hop(env, s | 1, peers) for s in combos(group)], 0)
+    mixed, kept, at = pl.pallas_call(
         functools.partial(mix_kernel, peers),
         out_shape=(
             jax.ShapeDtypeStruct((secs, terms, vecs * width, wide), jnp.bfloat16),
-            jax.ShapeDtypeStruct(right_env.shape, right_env.dtype),
+            jax.ShapeDtypeStruct(env.shape, env.dtype),
             jax.ShapeDtypeStruct(target_slot.shape, jnp.int32),
         ),
-        in_specs=[pl.BlockSpec(memory_space=pltpu.HBM)] * 5,
+        in_specs=[pl.BlockSpec(memory_space=pltpu.HBM)] * 4 + [pl.BlockSpec(memory_space=pltpu.VMEM)],
         scratch_shapes=[
             pltpu.VMEM(left_env.shape, jnp.bfloat16),
             pltpu.VMEM(vectors.shape, jnp.bfloat16),
             pltpu.VMEM(dest.shape, jnp.int32),
             pltpu.VMEM(target_slot.shape, jnp.int32),
-            pltpu.SemaphoreType.DMA((6,)),
+            pltpu.SemaphoreType.DMA((5,)),
         ],
         compiler_params=pltpu.CompilerParams(vmem_limit_bytes=16 * 2**20),
         cost_estimate=pl.CostEstimate(
@@ -153,12 +159,15 @@
             bytes_accessed=6 * vecs * secs * width * wide,
             transcendentals=0,
         ),
-    )(*[pltpu.with_memory_space_constraint(x, pltpu.HBM) for x in (left_env, vectors, right_env, dest, target_slot)])
-    env, kept = right_env, own
-    for group in phases_of(peers):
-        env = kept = jnp.concatenate([kept] + [hop(env, s | 1, peers) for s in combos(group)], 0)
+    )(*[pltpu.with_memory_space_constraint(x, pltpu.HBM) for x in (left_env, vectors, dest, target_slot)], env)
+    for group in groups[1:]:
+        pieces = [kept] + [hop(env, s | 1, peers) for s in combos(group)]
+        half = len(pieces) // 2
+        pieces = pieces[half:] + pieces[:half]
+        env = kept = jnp.concatenate(pieces, 0)
     if peers > 1:
-        env = jnp.concatenate([env, hop(env, 1, peers)], 0)
+        half = env.shape[0] // 2
+        env = jnp.concatenate([env, hop(env[:half], 1, peers), hop(env[half:], 1, peers)], 0)
     return pl.pallas_call(
         close_kernel,
         out_shape=jax.ShapeDtypeStruct(vectors.shape, jnp.bfloat16),

time: 16.2 us -> 16 us (0.988)
  waiting for transfers between devices: 5.42 us -> 4.1 us
  local copies, waits for them, and re-layouts: 0.16 us -> 0.89 us
  starting transfers between devices: 7.1 us -> 7.4 us
    ppermute x5 -> x6, waiting for transfers between devices: 5.42 us -> 4.1 us  [hop(): return lax.ppermute(x, 'sec', [(i, i ^ apart) for i in range(peers)])]
    unnamed x4 -> x6, local copies, waits for them, and re-layouts: 0.09 us -> 0.86 us
    ppermute x5 -> x6, starting transfers between devices: 7.1 us -> 7.4 us  [hop(): return lax.ppermute(x, 'sec', [(i, i ^ apart) for i in range(peers)])]
  transfers between devices with their start and end apart: 5 -> 6, of which waited for: 5 -> 6; matrix products, arithmetic and copies ran while one was open for 0% -> 6% of each run, Pallas kernels for 12% -> 12%
where the time goes in v5:
time: 16 us; the launch traced here: 15.8 us
  starting transfers between devices  7.4 us (46%)
  waiting for transfers between devices  4.1 us (26%)
  Pallas kernels  3.34 us (21%)
  local copies, waits for them, and re-layouts  0.89 us (6%)
    ppermute x6, starting transfers between devices, hop(): return lax.ppermute(x, 'sec', [(i, i ^ apart) for i in range(peers)])  7.4 us
    ppermute x6, waiting for transfers between devices, hop(): return lax.ppermute(x, 'sec', [(i, i ^ apart) for i in range(peers)])  4.1 us
    pallas_call x1, Pallas kernels, body(): pl.pallas_call(functools.partial(mix_kernel, peers), out_shape=(jax.Shape...  1.86 us
    pallas_call x1, Pallas kernels, body(): pl.pallas_call(close_kernel, out_shape=jax.ShapeDtypeStruct(vectors.shape...  1.48 us
    unnamed x6, local copies, waits for them, and re-layouts  0.86 us
  transfers between devices with their start and end apart: 6, of which 6 were waited for; matrix products, arithmetic and copies ran while one was open for 6% of the time, Pallas kernels for 12%

profile of v5, /device:TPU:0, one launch (start us, length us, event | category | flops | bytes accessed | tf_op | source)
XLA Modules:
  0.0 15.8 jit_solution(17803585268172286203)
XLA Ops:
  0.0 3.5 %collective-permute-start = (bf16[2,64,128]{2,1,0:T(8,128)(2,1)}, bf16[2,64,128]{2,1,0:T(8,128)(2,1)S(1)}, u32[]{:S(2)}, u32[]{:S(2)}) collective-permute-start(bf16[2,64,128]{2,1,0:T(8,128)(2,1)} %param.7), channel_id=1, source_target_pairs={{0,9},{1,8},{2,11},{3,10},{4,13},{5,12},{6,15},{7,14},{8,1},{9,0},... | collective-permute-start | bytes 98312 | tf_op jit(solution)/shard_map/ppermute | solution.py:61
  3.5 0.8 %constant_dynamic-update-slice_fusion.1 = bf16[4,64,128]{2,1,0:T(8,128)(2,1)S(1)} fusion(bf16[2,64,128]{2,1,0:T(8,128)(2,1)} %param.7), kind=kLoop, calls=%fused_computation.3 | loop fusion | bytes 65536
  4.3 1.3 %collective-permute-done = bf16[2,64,128]{2,1,0:T(8,128)(2,1)S(1)} collective-permute-done((bf16[2,64,128]{2,1,0:T(8,128)(2,1)}, bf16[2,64,128]{2,1,0:T(8,128)(2,1)S(1)}, u32[]{:S(2)}, u32[]{:S(2)}) %collective-permute-start) | collective-permute-done | bytes 32800 | tf_op jit(solution)/shard_map/ppermute | solution.py:61
  5.6 1.6 %collective-permute-start.2 = (bf16[4,64,128]{2,1,0:T(8,128)(2,1)S(1)}, bf16[4,64,128]{2,1,0:T(8,128)(2,1)S(1)}, u32[]{:S(2)}, u32[]{:S(2)}) collective-permute-start(bf16[4,64,128]{2,1,0:T(8,128)(2,1)S(1)} %constant_dynamic-update-slice_fusion.env_ref), channel_id=1, source_target_pairs={{0,3},{1,2},{2,1},{3,0},{4,7},{5,6},{6,5},{7,4},{8,11},{9,10},{10,... | collective-permute-start | bytes 196616 | tf_op jit(solution)/shard_map/ppermute | solution.py:61
  7.2 1.5 %collective-permute-start.1 = (bf16[4,64,128]{2,1,0:T(8,128)(2,1)S(1)}, bf16[4,64,128]{2,1,0:T(8,128)(2,1)S(1)}, u32[]{:S(2)}, u32[]{:S(2)}) collective-permute-start(bf16[4,64,128]{2,1,0:T(8,128)(2,1)S(1)} %constant_dynamic-update-slice_fusion.env_ref), channel_id=1, source_target_pairs={{0,7},{1,6},{2,5},{3,4},{4,3},{5,2},{6,1},{7,0},{8,15},{9,14},{10,... | collective-permute-start | bytes 196616 | tf_op jit(solution)/shard_map/ppermute | solution.py:61
  8.8 0.1 collective-permute-start.3
  8.8 1.9 %shard_map.55 = (bf16[2,2,192,1024]{3,2,1,0:T(8,128)(2,1)S(1)}, bf16[4,64,128]{2,1,0:T(8,128)(2,1)S(1)}, s32[2,16]{1,0:T(2,128)S(1)}) custom-call(bf16[2,64,128]{2,1,0:T(8,128)(2,1)} %left_hbm.1, bf16[3,2,64,1024]{3,2,1,0:T(8,128)(2,1)} %vec_hbm.1, s32[2,16]{1,0:T(2,128)} %bitcast.1, s32[2,16]{1,0:T(2,128)} %slot_hbm.1, ...), custom_call_target="tpu_custom_call" | custom-call | flops 100663296 | bytes 2359296 | tf_op jit(solution)/shard_map/pallas_call | solution.py:141
  10.7 0.1 collective-permute-done.2
  10.9 1.1 %collective-permute-done.1 = bf16[4,64,128]{2,1,0:T(8,128)(2,1)S(1)} collective-permute-done((bf16[4,64,128]{2,1,0:T(8,128)(2,1)S(1)}, bf16[4,64,128]{2,1,0:T(8,128)(2,1)S(1)}, u32[]{:S(2)}, u32[]{:S(2)}) %collective-permute-start.1) | collective-permute-done | bytes 65568 | tf_op jit(solution)/shard_map/ppermute | solution.py:61
  12.0 0.4 %collective-permute-start.4 = (bf16[8,64,128]{2,1,0:T(8,128)(2,1)S(1)}, bf16[8,64,128]{2,1,0:T(8,128)(2,1)S(1)}, u32[]{:S(2)}, u32[]{:S(2)}) collective-permute-start(bf16[8,64,128]{2,1,0:T(8,128)(2,1)S(1)} %pad_maximum_fusion), channel_id=1, source_target_pairs={{0,1},{1,0},{2,3},{3,2},{4,5},{5,4},{6,7},{7,6},{8,9},{9,8},{10,11... | collective-permute-start | bytes 393224 | tf_op jit(solution)/shard_map/ppermute | solution.py:61
  12.4 0.4 %collective-permute-done.3 = bf16[4,64,128]{2,1,0:T(8,128)(2,1)S(1)} collective-permute-done((bf16[4,64,128]{2,1,0:T(8,128)(2,1)S(1)}, bf16[4,64,128]{2,1,0:T(8,128)(2,1)S(1)}, u32[]{:S(2)}, u32[]{:S(2)}) %collective-permute-start.3) | collective-permute-done | bytes 65568 | tf_op jit(solution)/shard_map/ppermute | solution.py:61
  12.9 0.2 %collective-permute-start.5 = (bf16[8,64,128]{2,1,0:T(8,128)(2,1)S(1)}, bf16[8,64,128]{2,1,0:T(8,128)(2,1)S(1)}, u32[]{:S(2)}, u32[]{:S(2)}) collective-permute-start(bf16[8,64,128]{2,1,0:T(8,128)(2,1)S(1)} %pad_maximum_fusion.1), channel_id=1, source_target_pairs={{0,1},{1,0},{2,3},{3,2},{4,5},{5,4},{6,7},{7,6},{8,9},{9,8},{10,11... | collective-permute-start | bytes 393224 | tf_op jit(solution)/shard_map/ppermute | solution.py:61
  13.1 0.3 %collective-permute-done.4 = bf16[8,64,128]{2,1,0:T(8,128)(2,1)S(1)} collective-permute-done((bf16[8,64,128]{2,1,0:T(8,128)(2,1)S(1)}, bf16[8,64,128]{2,1,0:T(8,128)(2,1)S(1)}, u32[]{:S(2)}, u32[]{:S(2)}) %collective-permute-start.4) | collective-permute-done | bytes 131104 | tf_op jit(solution)/shard_map/ppermute | solution.py:61
  13.4 0.9 %collective-permute-done.5 = bf16[8,64,128]{2,1,0:T(8,128)(2,1)S(1)} collective-permute-done((bf16[8,64,128]{2,1,0:T(8,128)(2,1)S(1)}, bf16[8,64,128]{2,1,0:T(8,128)(2,1)S(1)}, u32[]{:S(2)}, u32[]{:S(2)}) %collective-permute-start.5) | collective-permute-done | bytes 131104 | tf_op jit(solution)/shard_map/ppermute | solution.py:61
  14.3 1.5 %shard_map.56 = bf16[3,2,64,1024]{3,2,1,0:T(8,128)(2,1)} custom-call(s32[2,16]{1,0:T(2,128)S(1)} %get-tuple-element.8.at_ref, bf16[2,2,192,1024]{3,2,1,0:T(8,128)(2,1)S(1)} %get-tuple-element.9.mixed_ref, bf16[32,64,128]{2,1,0:T(8,128)(2,1)S(1)} %constant_dynamic-update-slice_fusion.2.env_ref), custom_call_target="tpu_custom_call" | custom-call | flops 100663296 | bytes 2359296 | tf_op jit(solution)/shard_map/pallas_call | solution.py:171
  (9 shorter events, 0.1 us)
Async XLA Ops:
  0.0 5.6 %collective-permute-start = (bf16[2,64,128]{2,1,0:T(8,128)(2,1)}, bf16[2,64,128]{2,1,0:T(8,128)(2,1)S(1)}, u32[]{:S(2)}, u32[]{:S(2)}) collective-permute-start(bf16[2,64,128]{2,1,0:T(8,128)(2,1)} %param.7), channel_id=1, source_target_pairs={{0,9},{1,8},{2,11},{3,10},{4,13},{5,12},{6,15},{7,14},{8,1},{9,0},... | collective-permute-start | bytes 98312 | tf_op jit(solution)/shard_map/ppermute | solution.py:61
  5.6 5.3 %collective-permute-start.2 = (bf16[4,64,128]{2,1,0:T(8,128)(2,1)S(1)}, bf16[4,64,128]{2,1,0:T(8,128)(2,1)S(1)}, u32[]{:S(2)}, u32[]{:S(2)}) collective-permute-start(bf16[4,64,128]{2,1,0:T(8,128)(2,1)S(1)} %constant_dynamic-update-slice_fusion.env_ref), channel_id=1, source_target_pairs={{0,3},{1,2},{2,1},{3,0},{4,7},{5,6},{6,5},{7,4},{8,11},{9,10},{10,... | collective-permute-start | bytes 196616 | tf_op jit(solution)/shard_map/ppermute | solution.py:61
  7.2 4.7 %collective-permute-start.1 = (bf16[4,64,128]{2,1,0:T(8,128)(2,1)S(1)}, bf16[4,64,128]{2,1,0:T(8,128)(2,1)S(1)}, u32[]{:S(2)}, u32[]{:S(2)}) collective-permute-start(bf16[4,64,128]{2,1,0:T(8,128)(2,1)S(1)} %constant_dynamic-update-slice_fusion.env_ref), channel_id=1, source_target_pairs={{0,7},{1,6},{2,5},{3,4},{4,3},{5,2},{6,1},{7,0},{8,15},{9,14},{10,... | collective-permute-start | bytes 196616 | tf_op jit(solution)/shard_map/ppermute | solution.py:61
  8.8 4.1 %collective-permute-start.3 = (bf16[4,64,128]{2,1,0:T(8,128)(2,1)S(1)}, bf16[4,64,128]{2,1,0:T(8,128)(2,1)S(1)}, u32[]{:S(2)}, u32[]{:S(2)}) collective-permute-start(bf16[4,64,128]{2,1,0:T(8,128)(2,1)S(1)} %constant_dynamic-update-slice_fusion.env_ref), channel_id=1, source_target_pairs={{0,5},{1,4},{2,7},{3,6},{4,1},{5,0},{6,3},{7,2},{8,13},{9,12},{10,... | collective-permute-start | bytes 196616 | tf_op jit(solution)/shard_map/ppermute | solution.py:61
  12.0 1.4 %collective-permute-start.4 = (bf16[8,64,128]{2,1,0:T(8,128)(2,1)S(1)}, bf16[8,64,128]{2,1,0:T(8,128)(2,1)S(1)}, u32[]{:S(2)}, u32[]{:S(2)}) collective-permute-start(bf16[8,64,128]{2,1,0:T(8,128)(2,1)S(1)} %pad_maximum_fusion), channel_id=1, source_target_pairs={{0,1},{1,0},{2,3},{3,2},{4,5},{5,4},{6,7},{7,6},{8,9},{9,8},{10,11... | collective-permute-start | bytes 393224 | tf_op jit(solution)/shard_map/ppermute | solution.py:61
  12.9 1.4 %collective-permute-start.5 = (bf16[8,64,128]{2,1,0:T(8,128)(2,1)S(1)}, bf16[8,64,128]{2,1,0:T(8,128)(2,1)S(1)}, u32[]{:S(2)}, u32[]{:S(2)}) collective-permute-start(bf16[8,64,128]{2,1,0:T(8,128)(2,1)S(1)} %pad_maximum_fusion.1), channel_id=1, source_target_pairs={{0,1},{1,0},{2,3},{3,2},{4,5},{5,4},{6,7},{7,6},{8,9},{9,8},{10,11... | collective-permute-start | bytes 393224 | tf_op jit(solution)/shard_map/ppermute | solution.py:61

commit v6 on v5

--- a/solution.py
+++ b/solution.py
@@ -8,53 +8,41 @@
 from jax.sharding import PartitionSpec as P
 
 
-def phases_of(peers):
+def bits_of(peers):
     bits = []
     bit = peers // 2
     while bit > 1:
         bits.append(bit)
         bit //= 2
-    groups = [[(bits[0], bits[0])]] if bits else []
-    for i in range(1, len(bits), 2):
-        if i + 1 == len(bits):
-            groups.append([(bits[i], bits[i])])
-        else:
-            high, low = bits[i], bits[i + 1]
-            groups.append([(high, high | low), (high | low, low)])
-    return groups
+    return bits
 
 
-def combos(group):
-    sums = [0]
-    for mask, _ in group:
-        sums = sums + [s ^ mask for s in sums]
-    return sums[1:]
+def shift(blocks, step):
+    return [x ^ step for x in blocks]
 
 
-def parity(x, test):
-    total, bit = 0, 1
-    while bit <= test:
-        if test & bit:
-            total = total ^ ((x // bit) & 1)
-        bit *= 2
-    return total
+def layout_of(peers):
+    bits = bits_of(peers)
+    blocks = [0] + [bit | 1 for bit in bits[:1]]
+    if len(bits) == 3:
+        first, high, low = [bit | 1 for bit in bits]
+        both = (bits[1] ^ bits[2]) | 1
+        early = [low] + shift([0, first], both) + blocks
+        late = [low ^ first] + shift([0, first], high)
+        blocks = early + late
+    else:
+        for bit in bits[1:]:
+            blocks = blocks + shift(blocks, bit | 1)
+    if peers > 1:
+        blocks = blocks + shift(blocks, 1)
+    return blocks
 
 
 def place_of(apart, peers):
-    place = 0
-    at = 0
-    flips = apart & 1
-    for turn, group in enumerate(phases_of(peers)):
-        some = 0
-        for mask, test in group:
-            own = parity(apart, test)
-            place = place + (own << at)
-            some = some | own
-            at += 1
-        if turn > 0:
-            place = place ^ (1 << (at - 1))
-        flips = flips ^ some
-    return place + (flips << at)
+    place = jnp.zeros_like(apart)
+    for at, x in enumerate(layout_of(peers)):
+        place = jnp.where(apart == x, at, place)
+    return place
 
 
 def hop(x, apart, peers):
@@ -64,10 +52,9 @@
 def mix_kernel(peers, left_hbm, vec_hbm, dest_hbm, slot_hbm, env_ref, mixed_ref, kept_ref, at_ref, left_ref, vec_ref, dest_ref, slot_ref, sems):
     copies = [
         pltpu.make_async_copy(left_hbm, left_ref, sems.at[0]),
-        pltpu.make_async_copy(vec_hbm.at[:, 0], vec_ref.at[:, 0], sems.at[1]),
-        pltpu.make_async_copy(vec_hbm.at[:, 1], vec_ref.at[:, 1], sems.at[2]),
-        pltpu.make_async_copy(dest_hbm, dest_ref, sems.at[3]),
-        pltpu.make_async_copy(slot_hbm, slot_ref, sems.at[4]),
+        pltpu.make_async_copy(vec_hbm, vec_ref, sems.at[1]),
+        pltpu.make_async_copy(dest_hbm, dest_ref, sems.at[2]),
+        pltpu.make_async_copy(slot_hbm, slot_ref, sems.at[3]),
     ]
     for copy in copies:
         copy.start()
@@ -134,10 +121,14 @@
     pairs = wide // width
     terms = left_env.shape[2] // width
     dest = target_device.reshape(secs, pairs)
-    groups = phases_of(peers)
+    bits = bits_of(peers)
     env = right_env
-    for group in groups[:1]:
-        env = jnp.concatenate([env] + [hop(env, s | 1, peers) for s in combos(group)], 0)
+    paired = len(bits) == 3
+    if bits:
+        far = hop(right_env, bits[0] | 1, peers)
+        if paired:
+            near = hop(right_env, bits[2] | 1, peers)
+        env = jnp.concatenate([right_env, far], 0)
     mixed, kept, at = pl.pallas_call(
         functools.partial(mix_kernel, peers),
         out_shape=(
@@ -151,7 +142,7 @@
             pltpu.VMEM(vectors.shape, jnp.bfloat16),
             pltpu.VMEM(dest.shape, jnp.int32),
             pltpu.VMEM(target_slot.shape, jnp.int32),
-            pltpu.SemaphoreType.DMA((5,)),
+            pltpu.SemaphoreType.DMA((4,)),
         ],
         compiler_params=pltpu.CompilerParams(vmem_limit_bytes=16 * 2**20),
         cost_estimate=pl.CostEstimate(
@@ -160,14 +151,18 @@
             transcendentals=0,
         ),
     )(*[pltpu.with_memory_space_constraint(x, pltpu.HBM) for x in (left_env, vectors, dest, target_slot)], env)
-    for group in groups[1:]:
-        pieces = [kept] + [hop(env, s | 1, peers) for s in combos(group)]
-        half = len(pieces) // 2
-        pieces = pieces[half:] + pieces[:half]
-        env = kept = jnp.concatenate(pieces, 0)
-    if peers > 1:
-        half = env.shape[0] // 2
-        env = jnp.concatenate([env, hop(env[:half], 1, peers), hop(env[half:], 1, peers)], 0)
+    if paired:
+        corner = hop(env, (bits[1] ^ bits[2]) | 1, peers)
+        side = hop(env, bits[1] | 1, peers)
+        rest = hop(far, bits[2] | 1, peers)
+        early = jnp.concatenate([near, corner, kept], 0)
+        late = jnp.concatenate([rest, side], 0)
+        env = jnp.concatenate([early, late, hop(early, 1, peers), hop(late, 1, peers)], 0)
+    else:
+        for bit in bits[1:]:
+            env = kept = jnp.concatenate([kept, hop(env, bit | 1, peers)], 0)
+        if peers > 1:
+            env = jnp.concatenate([kept, hop(env, 1, peers)], 0)
     return pl.pallas_call(
         close_kernel,
         out_shape=jax.ShapeDtypeStruct(vectors.shape, jnp.bfloat16),

time: 16 us -> 15.4 us (0.963)
  waiting for transfers between devices: 4.1 us -> 2.33 us
  starting transfers between devices: 7.4 us -> 8.55 us
    ppermute x6 -> x7, waiting for transfers between devices: 4.1 us -> 2.33 us  [hop(): return lax.ppermute(x, 'sec', [(i, i ^ apart) for i in range(peers)])]
    ppermute x6 -> x7, starting transfers between devices: 7.4 us -> 8.55 us  [hop(): return lax.ppermute(x, 'sec', [(i, i ^ apart) for i in range(peers)])]
    unnamed x6 -> x7, local copies, waits for them, and re-layouts: 0.86 us -> 0.87 us
  transfers between devices with their start and end apart: 6 -> 7, of which waited for: 6 -> 5; matrix products, arithmetic and copies ran while one was open for 6% -> 6% of each run, Pallas kernels for 12% -> 12%
where the time goes in v6:
time: 15.4 us; the launch traced here: 15.2 us
  starting transfers between devices  8.55 us (56%)
  Pallas kernels  3.35 us (22%)
  waiting for transfers between devices  2.33 us (15%)
  local copies, waits for them, and re-layouts  0.89 us (6%)
    ppermute x7, starting transfers between devices, hop(): return lax.ppermute(x, 'sec', [(i, i ^ apart) for i in range(peers)])  8.55 us
    ppermute x7, waiting for transfers between devices, hop(): return lax.ppermute(x, 'sec', [(i, i ^ apart) for i in range(peers)])  2.33 us
    pallas_call x1, Pallas kernels, body(): pl.pallas_call(functools.partial(mix_kernel, peers), out_shape=(jax.Shape...  1.87 us
    pallas_call x1, Pallas kernels, body(): pl.pallas_call(close_kernel, out_shape=jax.ShapeDtypeStruct(vectors.shape...  1.48 us
    unnamed x7, local copies, waits for them, and re-layouts  0.87 us
  transfers between devices with their start and end apart: 7, of which 5 were waited for; matrix products, arithmetic and copies ran while one was open for 6% of the time, Pallas kernels for 12%

profile of v6, /device:TPU:0, one launch (start us, length us, event | category | flops | bytes accessed | tf_op | source)
XLA Modules:
  0.0 15.2 jit_solution(6786772187620100006)
XLA Ops:
  0.0 3.5 %collective-permute-start = (bf16[2,64,128]{2,1,0:T(8,128)(2,1)}, bf16[2,64,128]{2,1,0:T(8,128)(2,1)S(1)}, u32[]{:S(2)}, u32[]{:S(2)}) collective-permute-start(bf16[2,64,128]{2,1,0:T(8,128)(2,1)} %param.7), channel_id=1, source_target_pairs={{0,9},{1,8},{2,11},{3,10},{4,13},{5,12},{6,15},{7,14},{8,1},{9,0},... | collective-permute-start | bytes 98312 | tf_op jit(solution)/shard_map/ppermute | solution.py:49
  3.5 1.8 %collective-permute-start.1 = (bf16[2,64,128]{2,1,0:T(8,128)(2,1)}, bf16[2,64,128]{2,1,0:T(8,128)(2,1)S(1)}, u32[]{:S(2)}, u32[]{:S(2)}) collective-permute-start(bf16[2,64,128]{2,1,0:T(8,128)(2,1)} %param.7), channel_id=1, source_target_pairs={{0,3},{1,2},{2,1},{3,0},{4,7},{5,6},{6,5},{7,4},{8,11},{9,10},{10,... | collective-permute-start | bytes 98312 | tf_op jit(solution)/shard_map/ppermute | solution.py:49
  5.2 0.8 %constant_dynamic-update-slice_fusion.1 = bf16[4,64,128]{2,1,0:T(8,128)(2,1)S(1)} fusion(bf16[2,64,128]{2,1,0:T(8,128)(2,1)} %param.7), kind=kLoop, calls=%fused_computation.3 | loop fusion | bytes 65536
  6.0 0.0 collective-permute-done
  6.1 2.2 %collective-permute-start.2 = (bf16[4,64,128]{2,1,0:T(8,128)(2,1)S(1)}, bf16[4,64,128]{2,1,0:T(8,128)(2,1)S(1)}, u32[]{:S(2)}, u32[]{:S(2)}) collective-permute-start(bf16[4,64,128]{2,1,0:T(8,128)(2,1)S(1)} %constant_dynamic-update-slice_fusion.env_ref), channel_id=1, source_target_pairs={{0,7},{1,6},{2,5},{3,4},{4,3},{5,2},{6,1},{7,0},{8,15},{9,14},{10,... | collective-permute-start | bytes 196616 | tf_op jit(solution)/shard_map/ppermute | solution.py:49
  8.2 0.5 %collective-permute-start.4 = (bf16[4,64,128]{2,1,0:T(8,128)(2,1)S(1)}, bf16[4,64,128]{2,1,0:T(8,128)(2,1)S(1)}, u32[]{:S(2)}, u32[]{:S(2)}) collective-permute-start(bf16[4,64,128]{2,1,0:T(8,128)(2,1)S(1)} %constant_dynamic-update-slice_fusion.env_ref), channel_id=1, source_target_pairs={{0,5},{1,4},{2,7},{3,6},{4,1},{5,0},{6,3},{7,2},{8,13},{9,12},{10,... | collective-permute-start | bytes 196616 | tf_op jit(solution)/shard_map/ppermute | solution.py:49
  8.7 0.2 %collective-permute-start.3 = (bf16[2,64,128]{2,1,0:T(8,128)(2,1)S(1)}, bf16[2,64,128]{2,1,0:T(8,128)(2,1)S(1)}, u32[]{:S(2)}, u32[]{:S(2)}) collective-permute-start(bf16[2,64,128]{2,1,0:T(8,128)(2,1)S(1)} %collective-permute-done), channel_id=1, source_target_pairs={{0,3},{1,2},{2,1},{3,0},{4,7},{5,6},{6,5},{7,4},{8,11},{9,10},{10,... | collective-permute-start | bytes 98312 | tf_op jit(solution)/shard_map/ppermute | solution.py:49
  8.9 1.9 %shard_map.55 = (bf16[2,2,192,1024]{3,2,1,0:T(8,128)(2,1)S(1)}, bf16[4,64,128]{2,1,0:T(8,128)(2,1)S(1)}, s32[2,16]{1,0:T(2,128)S(1)}) custom-call(bf16[2,64,128]{2,1,0:T(8,128)(2,1)} %left_hbm.1, bf16[3,2,64,1024]{3,2,1,0:T(8,128)(2,1)} %vec_hbm.1, s32[2,16]{1,0:T(2,128)} %bitcast.1, s32[2,16]{1,0:T(2,128)} %slot_hbm.1, ...), custom_call_target="tpu_custom_call" | custom-call | flops 100663296 | bytes 2359296 | tf_op jit(solution)/shard_map/pallas_call | solution.py:132
  10.8 0.0 collective-permute-done.1
  10.8 0.6 %collective-permute-done.2 = bf16[4,64,128]{2,1,0:T(8,128)(2,1)S(1)} collective-permute-done((bf16[4,64,128]{2,1,0:T(8,128)(2,1)S(1)}, bf16[4,64,128]{2,1,0:T(8,128)(2,1)S(1)}, u32[]{:S(2)}, u32[]{:S(2)}) %collective-permute-start.2) | collective-permute-done | bytes 65568 | tf_op jit(solution)/shard_map/ppermute | solution.py:49
  11.4 0.2 %collective-permute-start.5 = (bf16[10,64,128]{2,1,0:T(8,128)(2,1)S(1)}, bf16[10,64,128]{2,1,0:T(8,128)(2,1)S(1)}, u32[]{:S(2)}, u32[]{:S(2)}) collective-permute-start(bf16[10,64,128]{2,1,0:T(8,128)(2,1)S(1)} %pad_maximum_fusion), channel_id=1, source_target_pairs={{0,1},{1,0},{2,3},{3,2},{4,5},{5,4},{6,7},{7,6},{8,9},{9,8},{10,11... | collective-permute-start | bytes 491528 | tf_op jit(solution)/shard_map/ppermute | solution.py:49
  11.6 0.6 %collective-permute-done.3 = bf16[2,64,128]{2,1,0:T(8,128)(2,1)S(1)} collective-permute-done((bf16[2,64,128]{2,1,0:T(8,128)(2,1)S(1)}, bf16[2,64,128]{2,1,0:T(8,128)(2,1)S(1)}, u32[]{:S(2)}, u32[]{:S(2)}) %collective-permute-start.3) | collective-permute-done | bytes 32800 | tf_op jit(solution)/shard_map/ppermute | solution.py:49
  12.1 0.2 %collective-permute-done.4 = bf16[4,64,128]{2,1,0:T(8,128)(2,1)S(1)} collective-permute-done((bf16[4,64,128]{2,1,0:T(8,128)(2,1)S(1)}, bf16[4,64,128]{2,1,0:T(8,128)(2,1)S(1)}, u32[]{:S(2)}, u32[]{:S(2)}) %collective-permute-start.4) | collective-permute-done | bytes 65568 | tf_op jit(solution)/shard_map/ppermute | solution.py:49
  12.3 0.3 %collective-permute-start.6 = (bf16[6,64,128]{2,1,0:T(8,128)(2,1)S(1)}, bf16[6,64,128]{2,1,0:T(8,128)(2,1)S(1)}, u32[]{:S(2)}, u32[]{:S(2)}) collective-permute-start(bf16[6,64,128]{2,1,0:T(8,128)(2,1)S(1)} %pad_maximum_fusion.1), channel_id=1, source_target_pairs={{0,1},{1,0},{2,3},{3,2},{4,5},{5,4},{6,7},{7,6},{8,9},{9,8},{10,11... | collective-permute-start | bytes 294920 | tf_op jit(solution)/shard_map/ppermute | solution.py:49
  12.7 0.2 %collective-permute-done.5 = bf16[10,64,128]{2,1,0:T(8,128)(2,1)S(1)} collective-permute-done((bf16[10,64,128]{2,1,0:T(8,128)(2,1)S(1)}, bf16[10,64,128]{2,1,0:T(8,128)(2,1)S(1)}, u32[]{:S(2)}, u32[]{:S(2)}) %collective-permute-start.5) | collective-permute-done | bytes 163872 | tf_op jit(solution)/shard_map/ppermute | solution.py:49
  12.9 0.8 %collective-permute-done.6 = bf16[6,64,128]{2,1,0:T(8,128)(2,1)S(1)} collective-permute-done((bf16[6,64,128]{2,1,0:T(8,128)(2,1)S(1)}, bf16[6,64,128]{2,1,0:T(8,128)(2,1)S(1)}, u32[]{:S(2)}, u32[]{:S(2)}) %collective-permute-start.6) | collective-permute-done | bytes 98336 | tf_op jit(solution)/shard_map/ppermute | solution.py:49
  13.7 1.5 %shard_map.56 = bf16[3,2,64,1024]{3,2,1,0:T(8,128)(2,1)} custom-call(s32[2,16]{1,0:T(2,128)S(1)} %get-tuple-element.8.at_ref, bf16[2,2,192,1024]{3,2,1,0:T(8,128)(2,1)S(1)} %get-tuple-element.9.mixed_ref, bf16[32,64,128]{2,1,0:T(8,128)(2,1)S(1)} %constant_dynamic-update-slice_fusion.2.env_ref), custom_call_target="tpu_custom_call" | custom-call | flops 100663296 | bytes 2359296 | tf_op jit(solution)/shard_map/pallas_call | solution.py:166
  (10 shorter events, 0.1 us)
Async XLA Ops:
  0.0 6.0 %collective-permute-start = (bf16[2,64,128]{2,1,0:T(8,128)(2,1)}, bf16[2,64,128]{2,1,0:T(8,128)(2,1)S(1)}, u32[]{:S(2)}, u32[]{:S(2)}) collective-permute-start(bf16[2,64,128]{2,1,0:T(8,128)(2,1)} %param.7), channel_id=1, source_target_pairs={{0,9},{1,8},{2,11},{3,10},{4,13},{5,12},{6,15},{7,14},{8,1},{9,0},... | collective-permute-start | bytes 98312 | tf_op jit(solution)/shard_map/ppermute | solution.py:49
  3.5 7.3 %collective-permute-start.1 = (bf16[2,64,128]{2,1,0:T(8,128)(2,1)}, bf16[2,64,128]{2,1,0:T(8,128)(2,1)S(1)}, u32[]{:S(2)}, u32[]{:S(2)}) collective-permute-start(bf16[2,64,128]{2,1,0:T(8,128)(2,1)} %param.7), channel_id=1, source_target_pairs={{0,3},{1,2},{2,1},{3,0},{4,7},{5,6},{6,5},{7,4},{8,11},{9,10},{10,... | collective-permute-start | bytes 98312 | tf_op jit(solution)/shard_map/ppermute | solution.py:49
  6.1 5.3 %collective-permute-start.2 = (bf16[4,64,128]{2,1,0:T(8,128)(2,1)S(1)}, bf16[4,64,128]{2,1,0:T(8,128)(2,1)S(1)}, u32[]{:S(2)}, u32[]{:S(2)}) collective-permute-start(bf16[4,64,128]{2,1,0:T(8,128)(2,1)S(1)} %constant_dynamic-update-slice_fusion.env_ref), channel_id=1, source_target_pairs={{0,7},{1,6},{2,5},{3,4},{4,3},{5,2},{6,1},{7,0},{8,15},{9,14},{10,... | collective-permute-start | bytes 196616 | tf_op jit(solution)/shard_map/ppermute | solution.py:49
  8.2 4.1 %collective-permute-start.4 = (bf16[4,64,128]{2,1,0:T(8,128)(2,1)S(1)}, bf16[4,64,128]{2,1,0:T(8,128)(2,1)S(1)}, u32[]{:S(2)}, u32[]{:S(2)}) collective-permute-start(bf16[4,64,128]{2,1,0:T(8,128)(2,1)S(1)} %constant_dynamic-update-slice_fusion.env_ref), channel_id=1, source_target_pairs={{0,5},{1,4},{2,7},{3,6},{4,1},{5,0},{6,3},{7,2},{8,13},{9,12},{10,... | collective-permute-start | bytes 196616 | tf_op jit(solution)/shard_map/ppermute | solution.py:49
  8.7 3.4 %collective-permute-start.3 = (bf16[2,64,128]{2,1,0:T(8,128)(2,1)S(1)}, bf16[2,64,128]{2,1,0:T(8,128)(2,1)S(1)}, u32[]{:S(2)}, u32[]{:S(2)}) collective-permute-start(bf16[2,64,128]{2,1,0:T(8,128)(2,1)S(1)} %collective-permute-done), channel_id=1, source_target_pairs={{0,3},{1,2},{2,1},{3,0},{4,7},{5,6},{6,5},{7,4},{8,11},{9,10},{10,... | collective-permute-start | bytes 98312 | tf_op jit(solution)/shard_map/ppermute | solution.py:49
  11.4 1.5 %collective-permute-start.5 = (bf16[10,64,128]{2,1,0:T(8,128)(2,1)S(1)}, bf16[10,64,128]{2,1,0:T(8,128)(2,1)S(1)}, u32[]{:S(2)}, u32[]{:S(2)}) collective-permute-start(bf16[10,64,128]{2,1,0:T(8,128)(2,1)S(1)} %pad_maximum_fusion), channel_id=1, source_target_pairs={{0,1},{1,0},{2,3},{3,2},{4,5},{5,4},{6,7},{7,6},{8,9},{9,8},{10,11... | collective-permute-start | bytes 491528 | tf_op jit(solution)/shard_map/ppermute | solution.py:49
  12.3 1.4 %collective-permute-start.6 = (bf16[6,64,128]{2,1,0:T(8,128)(2,1)S(1)}, bf16[6,64,128]{2,1,0:T(8,128)(2,1)S(1)}, u32[]{:S(2)}, u32[]{:S(2)}) collective-permute-start(bf16[6,64,128]{2,1,0:T(8,128)(2,1)S(1)} %pad_maximum_fusion.1), channel_id=1, source_target_pairs={{0,1},{1,0},{2,3},{3,2},{4,5},{5,4},{6,7},{7,6},{8,9},{9,8},{10,11... | collective-permute-start | bytes 294920 | tf_op jit(solution)/shard_map/ppermute | solution.py:49

commit v7 on v6

--- a/solution.py
+++ b/solution.py
@@ -62,7 +62,8 @@
     for copy in copies:
         copy.wait()
     me = lax.axis_index("sec")
-    at_ref[...] = place_of(dest_ref[...] ^ me, peers) * vec_ref.shape[1] + slot_ref[...]
+    at = place_of(dest_ref[...] ^ me, peers) * vec_ref.shape[1] + slot_ref[...]
+    at_ref[...] = jnp.broadcast_to(at[:, :, None], at_ref.shape)
     vecs, secs, width, wide = vec_ref.shape
     low = lax.broadcasted_iota(jnp.int32, (width, wide), 1) % (2 * width) < width
 
@@ -91,7 +92,7 @@
     where = at_ref[...]
 
     def env_at(a, p):
-        return env_ref[where[a, p]]
+        return env_ref[where[a, p, 0]]
 
     for a in range(secs):
         for p in range(0, pairs, 2):
@@ -134,7 +135,7 @@
         out_shape=(
             jax.ShapeDtypeStruct((secs, terms, vecs * width, wide), jnp.bfloat16),
             jax.ShapeDtypeStruct(env.shape, env.dtype),
-            jax.ShapeDtypeStruct(target_slot.shape, jnp.int32),
+            jax.ShapeDtypeStruct((secs, pairs, 128), jnp.int32),
         ),
         in_specs=[pl.BlockSpec(memory_space=pltpu.HBM)] * 4 + [pl.BlockSpec(memory_space=pltpu.VMEM)],
         scratch_shapes=[

time: 15.4 us -> 15.3 us (level)
  no operation moved by 1% of the time
where the time goes in v7:
time: 15.3 us; the launch traced here: 15.1 us
  starting transfers between devices  8.55 us (56%)
  Pallas kernels  3.28 us (21%)
  waiting for transfers between devices  2.33 us (15%)
  local copies, waits for them, and re-layouts  0.89 us (6%)
    ppermute x7, starting transfers between devices, hop(): return lax.ppermute(x, 'sec', [(i, i ^ apart) for i in range(peers)])  8.55 us
    ppermute x7, waiting for transfers between devices, hop(): return lax.ppermute(x, 'sec', [(i, i ^ apart) for i in range(peers)])  2.33 us
    pallas_call x1, Pallas kernels, body(): pl.pallas_call(functools.partial(mix_kernel, peers), out_shape=(jax.Shape...  1.87 us
    pallas_call x1, Pallas kernels, body(): pl.pallas_call(close_kernel, out_shape=jax.ShapeDtypeStruct(vectors.shape...  1.41 us
    unnamed x7, local copies, waits for them, and re-layouts  0.87 us
  transfers between devices with their start and end apart: 7, of which 5 were waited for; matrix products, arithmetic and copies ran while one was open for 6% of the time, Pallas kernels for 12%

profile of v7, /device:TPU:0, one launch (start us, length us, event | category | flops | bytes accessed | tf_op | source)
XLA Modules:
  0.0 15.1 jit_solution(10397669332732231500)
XLA Ops:
  0.0 3.5 %collective-permute-start = (bf16[2,64,128]{2,1,0:T(8,128)(2,1)}, bf16[2,64,128]{2,1,0:T(8,128)(2,1)S(1)}, u32[]{:S(2)}, u32[]{:S(2)}) collective-permute-start(bf16[2,64,128]{2,1,0:T(8,128)(2,1)} %param.7), channel_id=1, source_target_pairs={{0,9},{1,8},{2,11},{3,10},{4,13},{5,12},{6,15},{7,14},{8,1},{9,0},... | collective-permute-start | bytes 98312 | tf_op jit(solution)/shard_map/ppermute | solution.py:49
  3.5 1.8 %collective-permute-start.1 = (bf16[2,64,128]{2,1,0:T(8,128)(2,1)}, bf16[2,64,128]{2,1,0:T(8,128)(2,1)S(1)}, u32[]{:S(2)}, u32[]{:S(2)}) collective-permute-start(bf16[2,64,128]{2,1,0:T(8,128)(2,1)} %param.7), channel_id=1, source_target_pairs={{0,3},{1,2},{2,1},{3,0},{4,7},{5,6},{6,5},{7,4},{8,11},{9,10},{10,... | collective-permute-start | bytes 98312 | tf_op jit(solution)/shard_map/ppermute | solution.py:49
  5.2 0.8 %constant_dynamic-update-slice_fusion.1 = bf16[4,64,128]{2,1,0:T(8,128)(2,1)S(1)} fusion(bf16[2,64,128]{2,1,0:T(8,128)(2,1)} %param.7), kind=kLoop, calls=%fused_computation.3 | loop fusion | bytes 65536
  6.0 0.0 collective-permute-done
  6.1 2.2 %collective-permute-start.2 = (bf16[4,64,128]{2,1,0:T(8,128)(2,1)S(1)}, bf16[4,64,128]{2,1,0:T(8,128)(2,1)S(1)}, u32[]{:S(2)}, u32[]{:S(2)}) collective-permute-start(bf16[4,64,128]{2,1,0:T(8,128)(2,1)S(1)} %constant_dynamic-update-slice_fusion.env_ref), channel_id=1, source_target_pairs={{0,7},{1,6},{2,5},{3,4},{4,3},{5,2},{6,1},{7,0},{8,15},{9,14},{10,... | collective-permute-start | bytes 196616 | tf_op jit(solution)/shard_map/ppermute | solution.py:49
  8.2 0.5 %collective-permute-start.4 = (bf16[4,64,128]{2,1,0:T(8,128)(2,1)S(1)}, bf16[4,64,128]{2,1,0:T(8,128)(2,1)S(1)}, u32[]{:S(2)}, u32[]{:S(2)}) collective-permute-start(bf16[4,64,128]{2,1,0:T(8,128)(2,1)S(1)} %constant_dynamic-update-slice_fusion.env_ref), channel_id=1, source_target_pairs={{0,5},{1,4},{2,7},{3,6},{4,1},{5,0},{6,3},{7,2},{8,13},{9,12},{10,... | collective-permute-start | bytes 196616 | tf_op jit(solution)/shard_map/ppermute | solution.py:49
  8.7 0.2 %collective-permute-start.3 = (bf16[2,64,128]{2,1,0:T(8,128)(2,1)S(1)}, bf16[2,64,128]{2,1,0:T(8,128)(2,1)S(1)}, u32[]{:S(2)}, u32[]{:S(2)}) collective-permute-start(bf16[2,64,128]{2,1,0:T(8,128)(2,1)S(1)} %collective-permute-done), channel_id=1, source_target_pairs={{0,3},{1,2},{2,1},{3,0},{4,7},{5,6},{6,5},{7,4},{8,11},{9,10},{10,... | collective-permute-start | bytes 98312 | tf_op jit(solution)/shard_map/ppermute | solution.py:49
  8.9 1.9 %shard_map.55 = (bf16[2,2,192,1024]{3,2,1,0:T(8,128)(2,1)S(1)}, bf16[4,64,128]{2,1,0:T(8,128)(2,1)S(1)}, s32[2,16,128]{2,1,0:T(8,128)S(1)}) custom-call(bf16[2,64,128]{2,1,0:T(8,128)(2,1)} %left_hbm.1, bf16[3,2,64,1024]{3,2,1,0:T(8,128)(2,1)} %vec_hbm.1, s32[2,16]{1,0:T(2,128)} %bitcast.1, s32[2,16]{1,0:T(2,128)} %slot_hbm.1, ...), custom_call_target="tpu_custom_call" | custom-call | flops 100663296 | bytes 2359296 | tf_op jit(solution)/shard_map/pallas_call | solution.py:133
  10.8 0.0 collective-permute-done.1
  10.8 0.6 %collective-permute-done.2 = bf16[4,64,128]{2,1,0:T(8,128)(2,1)S(1)} collective-permute-done((bf16[4,64,128]{2,1,0:T(8,128)(2,1)S(1)}, bf16[4,64,128]{2,1,0:T(8,128)(2,1)S(1)}, u32[]{:S(2)}, u32[]{:S(2)}) %collective-permute-start.2) | collective-permute-done | bytes 65568 | tf_op jit(solution)/shard_map/ppermute | solution.py:49
  11.4 0.2 %collective-permute-start.5 = (bf16[10,64,128]{2,1,0:T(8,128)(2,1)S(1)}, bf16[10,64,128]{2,1,0:T(8,128)(2,1)S(1)}, u32[]{:S(2)}, u32[]{:S(2)}) collective-permute-start(bf16[10,64,128]{2,1,0:T(8,128)(2,1)S(1)} %pad_maximum_fusion), channel_id=1, source_target_pairs={{0,1},{1,0},{2,3},{3,2},{4,5},{5,4},{6,7},{7,6},{8,9},{9,8},{10,11... | collective-permute-start | bytes 491528 | tf_op jit(solution)/shard_map/ppermute | solution.py:49
  11.6 0.6 %collective-permute-done.3 = bf16[2,64,128]{2,1,0:T(8,128)(2,1)S(1)} collective-permute-done((bf16[2,64,128]{2,1,0:T(8,128)(2,1)S(1)}, bf16[2,64,128]{2,1,0:T(8,128)(2,1)S(1)}, u32[]{:S(2)}, u32[]{:S(2)}) %collective-permute-start.3) | collective-permute-done | bytes 32800 | tf_op jit(solution)/shard_map/ppermute | solution.py:49
  12.1 0.2 %collective-permute-done.4 = bf16[4,64,128]{2,1,0:T(8,128)(2,1)S(1)} collective-permute-done((bf16[4,64,128]{2,1,0:T(8,128)(2,1)S(1)}, bf16[4,64,128]{2,1,0:T(8,128)(2,1)S(1)}, u32[]{:S(2)}, u32[]{:S(2)}) %collective-permute-start.4) | collective-permute-done | bytes 65568 | tf_op jit(solution)/shard_map/ppermute | solution.py:49
  12.3 0.3 %collective-permute-start.6 = (bf16[6,64,128]{2,1,0:T(8,128)(2,1)S(1)}, bf16[6,64,128]{2,1,0:T(8,128)(2,1)S(1)}, u32[]{:S(2)}, u32[]{:S(2)}) collective-permute-start(bf16[6,64,128]{2,1,0:T(8,128)(2,1)S(1)} %pad_maximum_fusion.1), channel_id=1, source_target_pairs={{0,1},{1,0},{2,3},{3,2},{4,5},{5,4},{6,7},{7,6},{8,9},{9,8},{10,11... | collective-permute-start | bytes 294920 | tf_op jit(solution)/shard_map/ppermute | solution.py:49
  12.7 0.2 %collective-permute-done.5 = bf16[10,64,128]{2,1,0:T(8,128)(2,1)S(1)} collective-permute-done((bf16[10,64,128]{2,1,0:T(8,128)(2,1)S(1)}, bf16[10,64,128]{2,1,0:T(8,128)(2,1)S(1)}, u32[]{:S(2)}, u32[]{:S(2)}) %collective-permute-start.5) | collective-permute-done | bytes 163872 | tf_op jit(solution)/shard_map/ppermute | solution.py:49
  12.9 0.8 %collective-permute-done.6 = bf16[6,64,128]{2,1,0:T(8,128)(2,1)S(1)} collective-permute-done((bf16[6,64,128]{2,1,0:T(8,128)(2,1)S(1)}, bf16[6,64,128]{2,1,0:T(8,128)(2,1)S(1)}, u32[]{:S(2)}, u32[]{:S(2)}) %collective-permute-start.6) | collective-permute-done | bytes 98336 | tf_op jit(solution)/shard_map/ppermute | solution.py:49
  13.7 1.4 %shard_map.56 = bf16[3,2,64,1024]{3,2,1,0:T(8,128)(2,1)} custom-call(s32[2,16,128]{2,1,0:T(8,128)S(1)} %get-tuple-element.8.at_ref, bf16[2,2,192,1024]{3,2,1,0:T(8,128)(2,1)S(1)} %get-tuple-element.9.mixed_ref, bf16[32,64,128]{2,1,0:T(8,128)(2,1)S(1)} %constant_dynamic-update-slice_fusion.2.env_ref), custom_call_target="tpu_custom_call" | custom-call | flops 100663296 | bytes 2359296 | tf_op jit(solution)/shard_map/pallas_call | solution.py:167
  (10 shorter events, 0.1 us)
Async XLA Ops:
  0.0 6.0 %collective-permute-start = (bf16[2,64,128]{2,1,0:T(8,128)(2,1)}, bf16[2,64,128]{2,1,0:T(8,128)(2,1)S(1)}, u32[]{:S(2)}, u32[]{:S(2)}) collective-permute-start(bf16[2,64,128]{2,1,0:T(8,128)(2,1)} %param.7), channel_id=1, source_target_pairs={{0,9},{1,8},{2,11},{3,10},{4,13},{5,12},{6,15},{7,14},{8,1},{9,0},... | collective-permute-start | bytes 98312 | tf_op jit(solution)/shard_map/ppermute | solution.py:49
  3.5 7.3 %collective-permute-start.1 = (bf16[2,64,128]{2,1,0:T(8,128)(2,1)}, bf16[2,64,128]{2,1,0:T(8,128)(2,1)S(1)}, u32[]{:S(2)}, u32[]{:S(2)}) collective-permute-start(bf16[2,64,128]{2,1,0:T(8,128)(2,1)} %param.7), channel_id=1, source_target_pairs={{0,3},{1,2},{2,1},{3,0},{4,7},{5,6},{6,5},{7,4},{8,11},{9,10},{10,... | collective-permute-start | bytes 98312 | tf_op jit(solution)/shard_map/ppermute | solution.py:49
  6.1 5.3 %collective-permute-start.2 = (bf16[4,64,128]{2,1,0:T(8,128)(2,1)S(1)}, bf16[4,64,128]{2,1,0:T(8,128)(2,1)S(1)}, u32[]{:S(2)}, u32[]{:S(2)}) collective-permute-start(bf16[4,64,128]{2,1,0:T(8,128)(2,1)S(1)} %constant_dynamic-update-slice_fusion.env_ref), channel_id=1, source_target_pairs={{0,7},{1,6},{2,5},{3,4},{4,3},{5,2},{6,1},{7,0},{8,15},{9,14},{10,... | collective-permute-start | bytes 196616 | tf_op jit(solution)/shard_map/ppermute | solution.py:49
  8.2 4.1 %collective-permute-start.4 = (bf16[4,64,128]{2,1,0:T(8,128)(2,1)S(1)}, bf16[4,64,128]{2,1,0:T(8,128)(2,1)S(1)}, u32[]{:S(2)}, u32[]{:S(2)}) collective-permute-start(bf16[4,64,128]{2,1,0:T(8,128)(2,1)S(1)} %constant_dynamic-update-slice_fusion.env_ref), channel_id=1, source_target_pairs={{0,5},{1,4},{2,7},{3,6},{4,1},{5,0},{6,3},{7,2},{8,13},{9,12},{10,... | collective-permute-start | bytes 196616 | tf_op jit(solution)/shard_map/ppermute | solution.py:49
  8.7 3.4 %collective-permute-start.3 = (bf16[2,64,128]{2,1,0:T(8,128)(2,1)S(1)}, bf16[2,64,128]{2,1,0:T(8,128)(2,1)S(1)}, u32[]{:S(2)}, u32[]{:S(2)}) collective-permute-start(bf16[2,64,128]{2,1,0:T(8,128)(2,1)S(1)} %collective-permute-done), channel_id=1, source_target_pairs={{0,3},{1,2},{2,1},{3,0},{4,7},{5,6},{6,5},{7,4},{8,11},{9,10},{10,... | collective-permute-start | bytes 98312 | tf_op jit(solution)/shard_map/ppermute | solution.py:49
  11.4 1.5 %collective-permute-start.5 = (bf16[10,64,128]{2,1,0:T(8,128)(2,1)S(1)}, bf16[10,64,128]{2,1,0:T(8,128)(2,1)S(1)}, u32[]{:S(2)}, u32[]{:S(2)}) collective-permute-start(bf16[10,64,128]{2,1,0:T(8,128)(2,1)S(1)} %pad_maximum_fusion), channel_id=1, source_target_pairs={{0,1},{1,0},{2,3},{3,2},{4,5},{5,4},{6,7},{7,6},{8,9},{9,8},{10,11... | collective-permute-start | bytes 491528 | tf_op jit(solution)/shard_map/ppermute | solution.py:49
  12.3 1.4 %collective-permute-start.6 = (bf16[6,64,128]{2,1,0:T(8,128)(2,1)S(1)}, bf16[6,64,128]{2,1,0:T(8,128)(2,1)S(1)}, u32[]{:S(2)}, u32[]{:S(2)}) collective-permute-start(bf16[6,64,128]{2,1,0:T(8,128)(2,1)S(1)} %pad_maximum_fusion.1), channel_id=1, source_target_pairs={{0,1},{1,0},{2,3},{3,2},{4,5},{5,4},{6,7},{7,6},{8,9},{9,8},{10,11... | collective-permute-start | bytes 294920 | tf_op jit(solution)/shard_map/ppermute | solution.py:49
